TPU v7x, 32 devices: a whole 2x2x4 slice. The times are simulated.
32 devices in a mesh: dp: 4 (over x, core), expert: 8 (over z, y).
Axes of the slice: x: 2, y: 2, z: 4, core: 2. Of those that a mesh axis runs over, the one named last changes fastest.
Arguments:
- tokens: bfloat16 [4096, 1024], P(('dp', 'expert')), may hold values from -6 to 6
- router: float32 [1024, 8], replicated, may hold values from -0.1875 to 0.1875
- expert_lists: int32 [4096, 4], P(('dp', 'expert')), may hold values from 0 to 7, as said below
- slot_positions: int32 [4096, 4], P(('dp', 'expert')), may hold values from 0 to 79, as said below
- teacher_gate: bfloat16 [1024, 2752], P(None, 'expert'), may hold values from -0.1875 to 0.1875
- teacher_up: bfloat16 [1024, 2752], P(None, 'expert'), may hold values from -0.1875 to 0.1875
- teacher_down: bfloat16 [2752, 1024], P('expert'), may hold values from -0.109375 to 0.109375
- expert_gate: bfloat16 [8, 1024, 704], P('expert'), may hold values from -0.1875 to 0.1875
- expert_up: bfloat16 [8, 1024, 704], P('expert'), may hold values from -0.1875 to 0.1875
- expert_down: bfloat16 [8, 704, 1024], P('expert'), may hold values from -0.21875 to 0.21875
Outputs:
- grad_gate: float32 [8, 1024, 704], P('expert', 'dp')
- grad_up: float32 [8, 1024, 704], P('expert', 'dp')
- grad_down: float32 [8, 704, 1024], P('expert', None, 'dp')
Inputs may be any that keep to these rules, and one draw needn't show every extreme that they name: `expert_lists`: the k-th expert of every token lies among k * 2 to (k + 1) * 2 - 1. The tokens of one device name each expert at most 80 times. For each index of dp and each such quarter of the experts, one expert is named exactly 80 times by the tokens of every device of that index. `slot_positions`: copies from the tokens of one device that name the same expert have distinct slots.
All inputs are finite; a program needn't handle non-finite values.
Results may differ from a plain program's by a relative error of at most 0.015.
Values may be sent and summed in bfloat16 or wider, within the bound.
A program may use at most 128 MiB of HBM per device.

v0:
```python
import math

import jax
import jax.numpy as jnp
from jax import lax
from jax.sharding import PartitionSpec as P


def silu_value(values):
    return values * jax.nn.sigmoid(values)


def teacher_rows(row_block, teacher_gate, teacher_up, teacher_down):
    pre_a = jnp.dot(row_block, teacher_gate, preferred_element_type=jnp.float32)
    pre_b = jnp.dot(row_block, teacher_up, preferred_element_type=jnp.float32)
    hidden_block = (silu_value(pre_a) * pre_b).astype(jnp.bfloat16)
    return jnp.dot(hidden_block, teacher_down, preferred_element_type=jnp.float32)


def make_term(group_tokens, teacher_gate, teacher_up, teacher_down):

    def teacher_term(first_row, row_count):
        return teacher_rows(group_tokens, teacher_gate, teacher_up, teacher_down)

    return teacher_term


def expert_forward(expert_rows, expert_gate, expert_up, expert_down):
    pre_gate = jnp.dot(expert_rows, expert_gate[0], preferred_element_type=jnp.float32)
    pre_up = jnp.dot(expert_rows, expert_up[0], preferred_element_type=jnp.float32)
    hidden = (silu_value(pre_gate) * pre_up).astype(jnp.bfloat16)
    output = jnp.dot(hidden, expert_down[0], preferred_element_type=jnp.float32).astype(
        jnp.bfloat16
    )
    return (pre_gate, pre_up, hidden, output)


def send_back(output_blocks):
    return lax.all_to_all(output_blocks, "expert", split_axis=0, concat_axis=0, tiled=True)


def on_device(
    tokens,
    router,
    expert_lists,
    slot_positions,
    teacher_gate,
    teacher_up,
    teacher_down,
    expert_gate,
    expert_up,
    expert_down,
):
    tok_count, model_width = tokens.shape
    top_count = expert_lists.shape[1]
    experts = router.shape[1]
    expert_devices = lax.axis_size("expert")
    data_devices = lax.axis_size("dp")
    capacity = 5 * tok_count // experts
    loss_scale = top_count / math.sqrt(
        tok_count * data_devices * expert_devices * top_count / experts
    )
    logits = jnp.dot(tokens.astype(jnp.float32), router, precision=lax.Precision.HIGHEST)
    chosen_mask = expert_lists[:, :, None] == jnp.arange(experts, dtype=jnp.int32)[None, None, :]
    picked = jnp.sum(jnp.where(chosen_mask, logits[:, None, :], 0.0), axis=2)
    sigmoid_pick = jax.nn.sigmoid(picked)
    weights = sigmoid_pick / jnp.sum(sigmoid_pick, axis=1, keepdims=True)
    position = expert_lists * capacity + slot_positions
    entry_index = (
        jnp.zeros((experts * capacity,), jnp.int32)
        .at[position.reshape(-1)]
        .set(jnp.arange(tok_count * top_count, dtype=jnp.int32) + 1)
    )
    filled = entry_index > 0
    entry_row = jnp.maximum(entry_index - 1, 0)
    group_tokens = lax.all_gather(tokens, "expert", axis=0, tiled=True)
    teacher_term = make_term(group_tokens, teacher_gate, teacher_up, teacher_down)
    target = lax.psum_scatter(
        teacher_term(jnp.int32(0), lax.axis_size("expert") * tok_count).astype(jnp.bfloat16),
        "expert",
        scatter_dimension=0,
        tiled=True,
    )
    lists_group, slots_group = (
        lax.all_gather(expert_lists, "expert", axis=0, tiled=True),
        lax.all_gather(slot_positions, "expert", axis=0, tiled=True),
    )
    my_expert = lax.axis_index("expert")
    group_count = lists_group.shape[0]
    source = (jnp.arange(group_count, dtype=jnp.int32) // tok_count)[:, None]
    local_slot = jnp.where(
        lists_group == my_expert, source * capacity + slots_group, expert_devices * capacity
    )
    owner_index = (
        jnp.zeros((expert_devices * capacity,), jnp.int32)
        .at[local_slot.reshape(-1)]
        .set(jnp.repeat(jnp.arange(group_count, dtype=jnp.int32) + 1, top_count), mode="drop")
    )
    expert_rows = jnp.where(
        (owner_index > 0)[:, None],
        group_tokens[jnp.maximum(owner_index - 1, 0)],
        jnp.zeros((), jnp.bfloat16),
    )
    pre_gate, pre_up, hidden, output = expert_forward(
        expert_rows, expert_gate, expert_up, expert_down
    )
    returned = send_back(output.reshape(expert_devices, capacity, model_width))
    flat_back = returned.reshape(experts * capacity, model_width)
    copies = flat_back[position]
    student = jnp.sum(weights[:, :, None] * copies.astype(jnp.float32), axis=1)
    scaled_error = (student - target.astype(jnp.float32)) * loss_scale
    cotangent = (
        (weights[:, :, None] * scaled_error[:, None, :])
        .astype(jnp.bfloat16)
        .reshape(tok_count * top_count, model_width)
    )
    cot_send = jnp.where(
        filled[:, None], cotangent[entry_row], jnp.zeros((), jnp.bfloat16)
    ).reshape(experts, capacity, model_width)
    cot_recv = lax.all_to_all(cot_send, "expert", split_axis=0, concat_axis=0, tiled=True).reshape(
        -1, model_width
    )
    grad_hidden = lax.dot_general(
        cot_recv, expert_down[0], (((1,), (1,)), ((), ())), preferred_element_type=jnp.float32
    )
    gate_sigmoid = jax.nn.sigmoid(pre_gate)
    grad_pre_gate = (
        grad_hidden * pre_up * gate_sigmoid * (1.0 + pre_gate * (1.0 - gate_sigmoid))
    ).astype(jnp.bfloat16)
    grad_pre_up = (grad_hidden * (pre_gate * gate_sigmoid)).astype(jnp.bfloat16)
    part_down = lax.dot_general(
        hidden, cot_recv, (((0,), (0,)), ((), ())), preferred_element_type=jnp.float32
    )
    part_gate = lax.dot_general(
        expert_rows, grad_pre_gate, (((0,), (0,)), ((), ())), preferred_element_type=jnp.float32
    )
    part_up = lax.dot_general(
        expert_rows, grad_pre_up, (((0,), (0,)), ((), ())), preferred_element_type=jnp.float32
    )
    sum_gate, sum_up = (
        lax.psum_scatter(
            part_gate.astype(jnp.bfloat16), "dp", scatter_dimension=0, tiled=True
        ).astype(jnp.float32),
        lax.psum_scatter(
            part_up.astype(jnp.bfloat16), "dp", scatter_dimension=0, tiled=True
        ).astype(jnp.float32),
    )
    sum_down = lax.psum_scatter(
        part_down.astype(jnp.bfloat16), "dp", scatter_dimension=1, tiled=True
    ).astype(jnp.float32)
    return (sum_gate[None], sum_up[None], sum_down[None])


def solution(mesh):
    return jax.shard_map(
        on_device,
        mesh=mesh,
        in_specs=(
            P(("dp", "expert"), None),
            P(),
            P(("dp", "expert"), None),
            P(("dp", "expert"), None),
            P(None, "expert"),
            P(None, "expert"),
            P("expert", None),
            P("expert", None, None),
            P("expert", None, None),
            P("expert", None, None),
        ),
        out_specs=(P("expert", "dp", None), P("expert", "dp", None), P("expert", None, "dp")),
        check_vma=False,
    )
```

profile of v0, /device:TPU:0, one launch (start us, length us, event | category | flops | bytes accessed | tf_op | source)
XLA Modules:
  0.0 309.8 jit_solution(4882061666486474567)
XLA Ops:
  7.2 0.7 all-gather.2.cloned.1.call-update
  8.0 28.1 %all_gather.10 = s32[1024,4]{0,1:T(4,128)S(1)} all-gather(s32[128,4]{0,1:T(4,128)} %param.13), channel_id=1, replica_groups=mesh['dp'=4,'expert'=8] {'expert'}, dimensions={0}, use_global_device_ids=true | all-gather | bytes 18432 | tf_op jit(solution)/shard_map/all_gather | solution.py:86
  36.1 26.4 %all_gather.9 = s32[1024,4]{0,1:T(4,128)S(1)} all-gather(s32[128,4]{0,1:T(4,128)} %param.12), channel_id=1, replica_groups=mesh['dp'=4,'expert'=8] {'expert'}, dimensions={0}, use_global_device_ids=true | all-gather | bytes 18432 | tf_op jit(solution)/shard_map/all_gather | solution.py:85
  62.5 0.2 copy.20
  62.7 0.3 reshape.141
  63.1 0.2 broadcast_in_dim.81
  63.3 0.3 reshape.181
  63.6 15.5 %scatter_custom_fusion = s32[640]{0:T(1024)S(1)} fusion(s32[4096]{0:T(1024)S(1)} %bitcast.46, s32[4096]{0:T(1024)S(1)} %reshape.181, s32[]{:T(128)} %constant.15.clone.1), kind=kCustom, calls=%fused_computation.61 | custom fusion | bytes 2564 | tf_op jit(solution)/shard_map/scatter | solution.py:97
  79.1 3.9 %fusion.23 = f32[1024,344]{0,1:T(8,128)} fusion(bf16[1024,1024]{1,0:T(8,128)(2,1)} %all-gather.2.cloned.1.call-done, bf16[1024,344]{0,1:T(8,128)(2,1)} %param.14), kind=kOutput, calls=%fused_computation.68 | convolution fusion | flops 721420288 | bytes 4210688 | tf_op jit(solution)/shard_map/dot_general | solution.py:14
  83.0 5.2 %convolution_convert_fusion = bf16[1024,1024]{1,0:T(8,128)(2,1)} fusion(bf16[344,1024]{1,0:T(8,128)(2,1)} %param.16, bf16[1024,1024]{1,0:T(8,128)(2,1)S(1)} %copy-done.1, bf16[1024,344]{0,1:T(8,128)(2,1)} %param.15, f32[1024,344]{0,1:T(8,128)} %fusion.23), kind=kOutput, calls=%fused_computation.7 | convolution fusion | flops 1446002688 | bytes 7012352 | tf_op jit(solution)/shard_map/dot_general | solution.py:17
  88.3 3.5 %gather_fusion = bf16[640,1024]{1,0:T(8,128)(2,1)} fusion(bf16[1024,1024]{1,0:T(8,128)(2,1)S(1)} %copy-done.1, s32[1024]{0:T(1024)S(1)} %pad_clamp_fusion.2), kind=kCustom, calls=%fused_computation | custom fusion | bytes 2624000 | tf_op jit(solution)/shard_map/gather | solution.py:101
  91.8 3.5 %fusion.6 = f32[640,704]{0,1:T(8,128)S(1)} fusion(bf16[1,1024,704]{1,2,0:T(8,128)(2,1)} %param.17, bf16[640,1024]{1,0:T(8,128)(2,1)} %gather_fusion, pred[640]{0:T(1024)(128)(4,1)S(1)} %broadcast_compare_fusion.1), kind=kOutput, calls=%fused_computation.23 | convolution fusion | flops 923402240 | bytes 4555392 | tf_op jit(solution)/shard_map/dot_general | solution.py:29
  95.3 2.7 multiply_convert_fusion.3
  98.0 2.3 convolution_convert_fusion.4
  100.3 3.7 %all-to-all-start = ((bf16[8,80,1024]{2,1,0:T(8,128)(2,1)}), bf16[8,80,1024]{2,1,0:T(8,128)(2,1)S(1)}, u32[]{:S(2)}, u32[]{:S(2)}) async-start(bf16[8,80,1024]{2,1,0:T(8,128)(2,1)} %bitcast.43), calls=%async_computation | async-start | bytes 2621440 | tf_op jit(solution)/shard_map/all_to_all | solution.py:39
  104.1 0.3 fusion.22
  104.5 0.1 copy.22
  104.6 0.1 reshape.149
  104.7 0.1 copy.24
  104.8 0.1 reshape.163
  105.0 0.1 copy.21
  105.1 0.1 reshape.143
  105.2 2.6 scatter_custom_fusion.1
  108.0 33.5 %all-to-all-done = bf16[8,80,1024]{2,1,0:T(8,128)(2,1)S(1)} async-done(((bf16[8,80,1024]{2,1,0:T(8,128)(2,1)}), bf16[8,80,1024]{2,1,0:T(8,128)(2,1)S(1)}, u32[]{:S(2)}, u32[]{:S(2)}) %all-to-all-start) | async-done | bytes 1310752 | tf_op jit(solution)/shard_map/all_to_all | solution.py:39
  141.5 2.8 gather_fusion.1
  144.3 1.7 reshape.197
  146.0 3.0 multiply_reduce_fusion
  149.0 19.7 %reduce-scatter.5.cloned.1.call-done = bf16[128,1024]{1,0:T(8,128)(2,1)} async-done(((bf16[1024,1024]{1,0:T(8,128)(2,1)}), bf16[128,1024]{1,0:T(8,128)(2,1)}) %reduce-scatter.5.cloned.1.call-update) | async-done | bytes 262160 | tf_op jit(solution)/shard_map/reduce_scatter | solution.py:78
  168.7 1.2 subtract_multiply_fusion
  169.9 0.6 mul.88
  170.5 1.8 mul.89
  172.2 1.8 multiply_convert_fusion
  174.0 3.5 %gather_fusion.2 = bf16[640,1024]{1,0:T(8,128)(2,1)} fusion(bf16[512,1024]{1,0:T(8,128)(2,1)S(1)} %multiply_convert_fusion, s32[1024]{0:T(1024)S(1)} %pad_clamp_fusion), kind=kCustom, calls=%fused_computation.2 | custom fusion | bytes 2624000 | tf_op jit(solution)/shard_map/gather | solution.py:118
  177.5 1.5 broadcast_select_fusion.1
  178.9 33.7 %all_to_all.10 = bf16[8,80,1024]{2,1,0:T(8,128)(2,1)S(1)} all-to-all(bf16[8,80,1024]{2,1,0:T(8,128)(2,1)S(1)} %broadcast_select_fusion.1), channel_id=1, replica_groups=mesh['dp'=4,'expert'=8] {'expert'}, dimensions={0} | all-to-all | bytes 2621440 | tf_op jit(solution)/shard_map/all_to_all | solution.py:120
  212.7 2.5 convolution_convert_fusion.3
  215.3 1.3 fusion.1
  216.6 1.2 copy-done.13
  217.8 0.1 copy-done.16
  217.9 2.8 convolution_convert_fusion.2
  220.8 1.4 copy-done.4
  222.2 4.7 %convolution_convert_fusion.1 = bf16[1024,704]{0,1:T(8,128)(2,1)} fusion(f32[640,704]{0,1:T(8,128)} %copy-done.13, f32[640,704]{0,1:T(8,128)} %copy-done.11, bf16[640,1024]{1,0:T(8,128)(2,1)S(1)} %copy-done.4, pred[640]{0:T(1024)(128)(4,1)S(1)} %broadcast_compare_fusion.1), kind=kOutput, calls=%fused_computation.13 | convolution fusion | flops 926826496 | bytes 6357632 | tf_op jit(solution)/shard_map/dot_general | solution.py:137
  226.9 14.7 %reduce-scatter.11.cloned.1.call-done = bf16[704,256]{1,0:T(8,128)(2,1)} async-done(((bf16[704,1024]{1,0:T(8,128)(2,1)}), bf16[704,256]{1,0:T(8,128)(2,1)}) %reduce-scatter.11.cloned.1.call-update) | async-done | bytes 360464 | tf_op jit(solution)/shard_map/reduce_scatter | solution.py:148
  241.6 1.9 bitcast_convert_fusion
  243.5 28.1 %reduce-scatter.7.cloned.1.call-done = bf16[256,704]{0,1:T(8,128)(2,1)} async-done(((bf16[1024,704]{0,1:T(8,128)(2,1)}), bf16[256,704]{0,1:T(8,128)(2,1)}) %reduce-scatter.7.cloned.1.call-update) | async-done | bytes 360464 | tf_op jit(solution)/shard_map/reduce_scatter | solution.py:141
  271.6 1.9 bitcast_convert_fusion.2
  273.5 27.9 %reduce-scatter.9.cloned.1.call-done = bf16[256,704]{0,1:T(8,128)(2,1)} async-done(((bf16[1024,704]{0,1:T(8,128)(2,1)}), bf16[256,704]{0,1:T(8,128)(2,1)}) %reduce-scatter.9.cloned.1.call-update) | async-done | bytes 360464 | tf_op jit(solution)/shard_map/reduce_scatter | solution.py:144
  301.4 1.9 bitcast_convert_fusion.1
  (59 shorter events, 0.6 us)
Async XLA Ops:
  7.2 90.8 %copy-start = (bf16[1,704,1024]{2,1,0:T(8,128)(2,1)S(1)}, bf16[1,704,1024]{2,1,0:T(8,128)(2,1)}, u32[]{:S(2)}) copy-start(bf16[1,704,1024]{2,1,0:T(8,128)(2,1)} %param.19) | copy-start | bytes 4325380
  7.2 71.9 %all-gather.2.cloned.1.call-start = ((), (), s32[]{:S(2)}) async-start(), calls=%async_computation.6 | async-start | bytes 2359296 | tf_op jit(solution)/shard_map/all_gather | solution.py:76
  7.9 160.8 %reduce-scatter.5.cloned.1.call-start = ((), (), s32[]{:S(2)}) async-start(), calls=%async_computation.7 | async-start | bytes 2359296 | tf_op jit(solution)/shard_map/reduce_scatter | solution.py:78
  79.1 3.9 %copy-start.1 = (bf16[1024,1024]{1,0:T(8,128)(2,1)S(1)}, bf16[1024,1024]{1,0:T(8,128)(2,1)}, u32[]{:S(2)}) copy-start(bf16[1024,1024]{1,0:T(8,128)(2,1)} %all-gather.2.cloned.1.call-done) | copy-start | bytes 6291460
  91.8 3.5 %copy-start.2 = (bf16[640,1024]{1,0:T(8,128)(2,1)S(1)}, bf16[640,1024]{1,0:T(8,128)(2,1)}, u32[]{:S(2)}) copy-start(bf16[640,1024]{1,0:T(8,128)(2,1)} %gather_fusion) | copy-start | bytes 3932164
  91.8 3.5 %copy-start.10 = (bf16[1,1024,704]{1,2,0:T(8,128)(2,1)S(1)}, bf16[1,1024,704]{1,2,0:T(8,128)(2,1)}, u32[]{:S(2)}) copy-start(bf16[1,1024,704]{1,2,0:T(8,128)(2,1)} %param.18) | copy-start | bytes 4325380
  95.3 2.7 copy-start.11
  98.0 2.3 copy-start.14
  100.3 3.8 %copy-start.5 = (bf16[128,1024]{1,0:T(8,128)(2,1)S(1)}, bf16[128,1024]{1,0:T(8,128)(2,1)}, u32[]{:S(2)}) copy-start(bf16[128,1024]{1,0:T(8,128)(2,1)} %param.10) | copy-start | bytes 786436
  100.3 3.8 %copy-start.7 = (f32[1024,8]{0,1:T(8,128)S(1)}, f32[1024,8]{0,1:T(8,128)}, u32[]{:S(2)}) copy-start(f32[1024,8]{0,1:T(8,128)} %param.11) | copy-start | bytes 98308
  100.3 4.1 %copy-start.8 = (s32[128,4]{0,1:T(4,128)S(1)}, s32[128,4]{0,1:T(4,128)}, u32[]{:S(2)}) copy-start(s32[128,4]{0,1:T(4,128)} %param.12) | copy-start | bytes 6148
  100.3 4.4 %copy-start.9 = (s32[128,4]{0,1:T(4,128)S(1)}, s32[128,4]{0,1:T(4,128)}, u32[]{:S(2)}) copy-start(s32[128,4]{0,1:T(4,128)} %param.13) | copy-start | bytes 6148
  100.3 41.2 %all-to-all-start = ((bf16[8,80,1024]{2,1,0:T(8,128)(2,1)}), bf16[8,80,1024]{2,1,0:T(8,128)(2,1)S(1)}, u32[]{:S(2)}, u32[]{:S(2)}) async-start(bf16[8,80,1024]{2,1,0:T(8,128)(2,1)} %bitcast.43), calls=%async_computation | async-start | bytes 2621440 | tf_op jit(solution)/shard_map/all_to_all | solution.py:39
  104.0 137.6 %reduce-scatter.11.cloned.1.call-start = ((), (), s32[]{:S(2)}) async-start(), calls=%async_computation.10 | async-start | bytes 1802240 | tf_op jit(solution)/shard_map/reduce_scatter | solution.py:148
  104.6 3.3 %copy-start.6 = (f32[128,4]{1,0:T(8,128)}, f32[128,4]{1,0:T(8,128)S(1)}, u32[]{:S(2)}) copy-start(f32[128,4]{1,0:T(8,128)S(1)} %copy.22) | copy-start | bytes 6148
  178.9 33.7 %copy-start.15 = (bf16[640,704]{0,1:T(8,128)(2,1)S(1)}, bf16[640,704]{0,1:T(8,128)(2,1)}, u32[]{:S(2)}) copy-start(bf16[640,704]{0,1:T(8,128)(2,1)} %copy-done.14) | copy-start | bytes 2703364
  215.2 56.4 %reduce-scatter.7.cloned.1.call-start = ((), (), s32[]{:S(2)}) async-start(), calls=%async_computation.8 | async-start | bytes 1802240 | tf_op jit(solution)/shard_map/reduce_scatter | solution.py:141
  215.2 2.6 copy-start.3
  215.2 2.6 copy-start.12
  215.2 2.7 copy-start.16
  216.6 1.2 copy-start.13
  220.7 1.5 copy-start.4
  220.7 80.6 %reduce-scatter.9.cloned.1.call-start = ((), (), s32[]{:S(2)}) async-start(), calls=%async_computation.9 | async-start | bytes 1802240 | tf_op jit(solution)/shard_map/reduce_scatter | solution.py:144
Sparse Core Ops, SparseCore 0:
  10.1 52.1 all-gather.1
  88.4 80.2 reduce-scatter.4
  215.3 26.2 reduce-scatter.10
  244.2 27.3 reduce-scatter.6
  274.0 27.3 reduce-scatter.8
where the time goes:
time: 310 us
  waiting for transfers between devices  125 us (40%)
  blocking collectives  88.2 us (28%)
  local copies, waits for them, and re-layouts  36.5 us (12%)
  matrix products  29.1 us (9%)
  between operations  14.1 us (5%)
  other arithmetic  13.3 us (4%)
  starting transfers between devices  3.92 us (1%)
    all_to_all x1, blocking collectives, on_device(): lax.all_to_all(cot_send, 'expert', split_axis=0, concat_axis=0, tiled=True)  33.7 us
    all_to_all x1, waiting for transfers between devices, send_back(): lax.all_to_all(output_blocks, 'expert', split_axis=0, concat_axis=0, tile...  33.5 us
    all_gather x1, blocking collectives, on_device(): lax.all_gather(slot_positions, 'expert', axis=0, tiled=True)  28.1 us
    reduce_scatter x1, waiting for transfers between devices, on_device(): lax.psum_scatter(part_gate.astype(jnp.bfloat16), 'dp', scatter_dimension=...  28.1 us
    reduce_scatter x1, waiting for transfers between devices, on_device(): lax.psum_scatter(part_up.astype(jnp.bfloat16), 'dp', scatter_dimension=0,...  27.9 us
    all_gather x1, blocking collectives, on_device(): lax.all_gather(expert_lists, 'expert', axis=0, tiled=True)  26.4 us
    reduce_scatter x1, waiting for transfers between devices, on_device(): lax.psum_scatter(teacher_term(jnp.int32(0), lax.axis_size('expert') * tok...  19.7 us
    scatter x1, local copies, waits for them, and re-layouts, on_device(): owner_index = jnp.zeros((expert_devices * capacity,), jnp.int32).at[local...  15.5 us
  transfers between devices with their start and end apart: 6, of which 5 were waited for; matrix products, arithmetic and copies ran while one was open for 17% of the time, Pallas kernels for 0%

commit v1 on v0

--- a/solution.py
+++ b/solution.py
@@ -1,8 +1,11 @@
+import functools
 import math
 
 import jax
 import jax.numpy as jnp
 from jax import lax
+from jax.experimental import pallas as pl
+from jax.experimental.pallas import tpu as pltpu
 from jax.sharding import PartitionSpec as P
 
 
@@ -151,9 +154,516 @@
     return (sum_gate[None], sum_up[None], sum_down[None])
 
 
+PAIR = 2
+BF16 = jnp.bfloat16
+F32 = jnp.float32
+
+
+def near_first(count):
+    return [sorted(range(count), key=lambda d, z=z: (abs(d - z), d < z if 2 * z < count else d > z)) for z in range(count)]
+
+
+def fused_kernel(
+    line,
+    data_devices,
+    loss_scale,
+    tokens_ref,
+    router_ref,
+    lists_ref,
+    tgate_hbm,
+    tup_hbm,
+    tdown_hbm,
+    gate_hbm,
+    up_hbm,
+    down_hbm,
+    out_gate,
+    out_up,
+    out_down,
+    tgate,
+    tup,
+    tdown,
+    egate,
+    eup,
+    edown,
+    rows_buf,
+    err_buf,
+    w_buf,
+    pre_gate,
+    pre_up,
+    hidden,
+    grad_pre_gate,
+    grad_pre_up,
+    cot,
+    part_own,
+    y_send,
+    y_recv,
+    z_send,
+    z_recv,
+    core_send,
+    core_recv,
+    core_send_d,
+    core_recv_d,
+    keep,
+    keep_d,
+    x_send,
+    x_recv,
+    x_send_d,
+    x_recv_d,
+    load_sem,
+    w_ssem,
+    w_rsem,
+    ag_rsem,
+    ag_ysem,
+    ag_zsem,
+    rs_ysem,
+    rs_yrsem,
+    rs_zsem,
+    rs_zrsem,
+    c_ssem,
+    c_rsem,
+    x_ssem,
+    x_rsem,
+):
+    tok_count, width = tokens_ref.shape
+    experts = router_ref.shape[1]
+    dp = lax.axis_index("dp")
+    me = lax.axis_index("expert")
+    z = me // PAIR
+    y = me % PAIR
+    peers = line * PAIR
+    pair_rows = PAIR * tok_count
+    y_peer = (dp, me + 1 - 2 * y)
+    x_at = dp // PAIR
+    core = dp % PAIR
+    core_peer = (dp + 1 - 2 * core, me)
+    x_peer = (dp + PAIR - 2 * PAIR * x_at, me)
+    table = near_first(line)
+
+    def order(step):
+        value = jnp.int32(0)
+        for at in range(line):
+            value = jnp.where(z == at, table[at][step], value)
+        return value
+
+    def remote(src, dst, ssem, rsem, device):
+        return pltpu.make_async_remote_copy(
+            src_ref=src,
+            dst_ref=dst,
+            send_sem=ssem,
+            recv_sem=rsem,
+            device_id=device,
+            device_id_type=pl.DeviceIdType.MESH,
+        )
+
+    barrier = pltpu.get_barrier_semaphore()
+    for step in range(1, peers):
+        pl.semaphore_signal(
+            barrier,
+            inc=1,
+            device_id=(dp, (me + step) % peers),
+            device_id_type=pl.DeviceIdType.MESH,
+        )
+    for device in (core_peer, x_peer):
+        pl.semaphore_signal(
+            barrier, inc=1, device_id=device, device_id_type=pl.DeviceIdType.MESH
+        )
+    loads = [
+        pltpu.make_async_copy(src, dst, load_sem.at[at])
+        for at, (src, dst) in enumerate(
+            (
+                (tgate_hbm, tgate),
+                (tup_hbm, tup),
+                (tdown_hbm, tdown),
+                (gate_hbm.at[0], egate),
+                (up_hbm.at[0], eup),
+                (down_hbm.at[0], edown),
+            )
+        )
+    ]
+    for load in loads:
+        load.start()
+
+    def block_of(buf, block):
+        return buf.at[pl.ds(pl.multiple_of(block * tok_count, tok_count), tok_count)]
+
+    block_of(rows_buf, me)[...] = tokens_ref[...]
+    pl.semaphore_wait(barrier, peers - 1 + 2)
+
+    def gather_start(buf, turn):
+        mine = block_of(buf, me)
+
+        @pl.when(z < line - 1)
+        def _():
+            remote(mine, mine, ag_zsem.at[turn, z], ag_rsem.at[turn, me], (dp, me + PAIR)).start()
+
+        @pl.when(z > 0)
+        def _():
+            remote(mine, mine, ag_zsem.at[turn, line], ag_rsem.at[turn, me], (dp, me - PAIR)).start()
+
+        remote(mine, mine, ag_ysem.at[turn, z], ag_rsem.at[turn, me], y_peer).start()
+
+    def away(d):
+        onward = jnp.where(d < z, z < line - 1, z > 0)
+        return onward, (dp, jnp.where(d < z, me + PAIR, me - PAIR))
+
+    def gather_rest(buf, turn, work):
+        def recv(block):
+            at = block_of(buf, block)
+            remote(at, at, ag_ysem.at[turn, 0], ag_rsem.at[turn, block], y_peer).wait_recv()
+
+        for step in range(1, line + 1):
+            if step < line:
+                d = order(step)
+                block = d * PAIR + y
+                recv(block)
+                at = block_of(buf, block)
+                onward, device = away(d)
+
+                @pl.when(onward)
+                def _():
+                    remote(
+                        at, at, ag_zsem.at[turn, d], ag_rsem.at[turn, block], device
+                    ).start()
+
+                remote(at, at, ag_ysem.at[turn, d], ag_rsem.at[turn, block], y_peer).start()
+            before = order(step - 1)
+            recv(before * PAIR + 1 - y)
+            work(before)
+
+    def gather_drain(buf, turn):
+        mine = block_of(buf, me)
+
+        @pl.when(z < line - 1)
+        def _():
+            remote(mine, mine, ag_zsem.at[turn, z], ag_rsem.at[turn, me], (dp, me + PAIR)).wait_send()
+
+        @pl.when(z > 0)
+        def _():
+            remote(mine, mine, ag_zsem.at[turn, line], ag_rsem.at[turn, me], (dp, me - PAIR)).wait_send()
+
+        for step in range(line):
+            d = order(step)
+            block = d * PAIR + y
+            at = block_of(buf, block)
+            if step:
+                onward, device = away(d)
+
+                @pl.when(onward)
+                def _():
+                    remote(
+                        at, at, ag_zsem.at[turn, d], ag_rsem.at[turn, block], device
+                    ).wait_send()
+
+            remote(at, at, ag_ysem.at[turn, d], ag_rsem.at[turn, block], y_peer).wait_send()
+
+    gather_start(rows_buf, 0)
+
+    logits = jnp.dot(
+        tokens_ref[...].astype(F32),
+        router_ref[...],
+        precision=lax.Precision.HIGHEST,
+        preferred_element_type=F32,
+    )
+    expert_ids = lax.broadcasted_iota(jnp.int32, (tok_count, experts), 1)
+    lists = lists_ref[...]
+    chosen = lists[:, 0:1] == expert_ids
+    for k in range(1, lists.shape[1]):
+        chosen = jnp.logical_or(chosen, lists[:, k : k + 1] == expert_ids)
+    picked = jnp.where(chosen, jax.nn.sigmoid(logits), 0.0)
+    weights = picked / jnp.sum(picked, axis=1, keepdims=True)
+    w_buf[me] = weights.T
+    w_copies = []
+    for step in range(1, peers):
+        copy = remote(
+            w_buf.at[me],
+            w_buf.at[me],
+            w_ssem.at[step - 1],
+            w_rsem.at[step - 1],
+            (dp, (me + step) % peers),
+        )
+        copy.start()
+        w_copies.append(copy)
+    for load in loads:
+        load.wait()
+    for copy in w_copies:
+        copy.wait()
+
+    def pair_weights(d):
+        columns = []
+        for part in range(PAIR):
+            table_part = w_buf[d * PAIR + part].T
+            columns.append(
+                jnp.sum(jnp.where(expert_ids == me, table_part, 0.0), axis=1, keepdims=True)
+            )
+        return jnp.concatenate(columns, axis=0)
+
+    def pair_of(d):
+        return pl.ds(pl.multiple_of(d * pair_rows, pair_rows), pair_rows)
+
+    def y_copy(d):
+        return remote(
+            y_send.at[d], y_recv.at[d], rs_ysem.at[d], rs_yrsem.at[d], y_peer
+        )
+
+    def forward(d):
+        where = pair_of(d)
+        rows = rows_buf[where, :]
+        pre_a = jnp.dot(rows, tgate[...], preferred_element_type=F32)
+        pre_b = jnp.dot(rows, tup[...], preferred_element_type=F32)
+        teacher_hidden = (silu_value(pre_a) * pre_b).astype(BF16)
+        teacher = jnp.dot(teacher_hidden, tdown[...], preferred_element_type=F32)
+        gate_values = jnp.dot(rows, egate[...], preferred_element_type=F32)
+        up_values = jnp.dot(rows, eup[...], preferred_element_type=F32)
+        pre_gate[where, :] = gate_values
+        pre_up[where, :] = up_values
+        hidden_values = (silu_value(gate_values) * up_values).astype(BF16)
+        hidden[where, :] = hidden_values
+        output = jnp.dot(hidden_values, edown[...], preferred_element_type=F32)
+        partial = pair_weights(d) * output - teacher
+        low = partial[:tok_count]
+        high = partial[tok_count:]
+        part_own[d] = jnp.where(y == 0, low, high)
+        y_send[d] = jnp.where(y == 0, high, low).astype(BF16)
+        y_copy(d).start()
+
+    gather_rest(rows_buf, 0, forward)
+
+    def z_copy(d):
+        rising = d > z
+        way = jnp.where(rising, 0, 1)
+        return remote(
+            z_send.at[d],
+            z_recv.at[way, d],
+            rs_zsem.at[d],
+            rs_zrsem.at[way, d],
+            (dp, jnp.where(rising, me + PAIR, me - PAIR)),
+        )
+
+    def z_arrived(way, d):
+        remote(
+            z_send.at[d], z_recv.at[way, d], rs_zsem.at[d], rs_zrsem.at[way, d], y_peer
+        ).wait_recv()
+        part_own[d] += z_recv[way, d].astype(F32)
+
+    for step in range(line - 1, -1, -1):
+        d = order(step)
+        y_copy(d).wait_recv()
+        part_own[d] += y_recv[d].astype(F32)
+
+        @pl.when(jnp.logical_and(d >= z, z > 0))
+        def _():
+            z_arrived(0, d)
+
+        @pl.when(jnp.logical_and(d <= z, z < line - 1))
+        def _():
+            z_arrived(1, d)
+
+        if step:
+            z_send[d] = part_own[d].astype(BF16)
+            z_copy(d).start()
+        else:
+            block_of(err_buf, me)[...] = (part_own[d] * loss_scale).astype(BF16)
+
+    gather_start(err_buf, 1)
+    gather_drain(rows_buf, 0)
+    for step in range(line):
+        d = order(step)
+        y_copy(d).wait_send()
+        if step:
+            z_copy(d).wait_send()
+
+    def backward(d):
+        where = pair_of(d)
+        cot_values = (pair_weights(d) * err_buf[where, :].astype(F32)).astype(BF16)
+        cot[where, :] = cot_values
+        grad_hidden = lax.dot_general(
+            cot_values, edown[...], (((1,), (1,)), ((), ())), preferred_element_type=F32
+        )
+        gate_values = pre_gate[where, :]
+        gate_sigmoid = jax.nn.sigmoid(gate_values)
+        grad_pre_gate[where, :] = (
+            grad_hidden
+            * pre_up[where, :]
+            * gate_sigmoid
+            * (1.0 + gate_values * (1.0 - gate_sigmoid))
+        ).astype(BF16)
+        grad_pre_up[where, :] = (grad_hidden * (gate_values * gate_sigmoid)).astype(BF16)
+
+    gather_rest(err_buf, 1, backward)
+
+    quarter = width // data_devices
+    contract = (((0,), (0,)), ((), ()))
+
+    def part(which, q):
+        columns = pl.ds(pl.multiple_of(q * quarter, quarter), quarter)
+        if which == 2:
+            return lax.dot_general(
+                hidden[...], cot[:, columns], contract, preferred_element_type=F32
+            )
+        grads = grad_pre_gate if which == 0 else grad_pre_up
+        return lax.dot_general(
+            rows_buf[:, columns], grads[...], contract, preferred_element_type=F32
+        )
+
+    def at_part(which, wide, tall):
+        return tall if which == 2 else wide.at[which]
+
+    def core_copy(which, slot):
+        return remote(
+            at_part(which, core_send, core_send_d).at[slot],
+            at_part(which, core_recv, core_recv_d).at[slot],
+            c_ssem.at[which, slot],
+            c_rsem.at[which, slot],
+            core_peer,
+        )
+
+    def x_copy(which):
+        return remote(
+            at_part(which, x_send, x_send_d),
+            at_part(which, x_recv, x_recv_d),
+            x_ssem.at[which],
+            x_rsem.at[which],
+            x_peer,
+        )
+
+    x_of = (1 - x_at, x_at)
+    for which in (0, 1, 2):
+        held = at_part(which, keep, keep_d)
+        sends = at_part(which, core_send, core_send_d)
+        recvs = at_part(which, core_recv, core_recv_d)
+        for slot in range(PAIR):
+            sends[slot] = part(which, x_of[slot] * PAIR + 1 - core).astype(BF16)
+            core_copy(which, slot).start()
+            own = part(which, x_of[slot] * PAIR + core)
+            core_copy(which, slot).wait_recv()
+            total = own + recvs[slot].astype(F32)
+            if slot == 0:
+                at_part(which, x_send, x_send_d)[...] = total.astype(BF16)
+                x_copy(which).start()
+            else:
+                held[...] = total
+    outs = (out_gate, out_up, out_down)
+    for which in (0, 1, 2):
+        x_copy(which).wait_recv()
+        outs[which][0] = (
+            at_part(which, keep, keep_d)[...] + at_part(which, x_recv, x_recv_d)[...].astype(F32)
+        )
+    gather_drain(err_buf, 1)
+    for which in (0, 1, 2):
+        x_copy(which).wait_send()
+        for slot in range(PAIR):
+            core_copy(which, slot).wait_send()
+
+
+def fused_on_device(
+    tokens,
+    router,
+    expert_lists,
+    slot_positions,
+    teacher_gate,
+    teacher_up,
+    teacher_down,
+    expert_gate,
+    expert_up,
+    expert_down,
+):
+    tok_count, width = tokens.shape
+    experts = router.shape[1]
+    top_count = expert_lists.shape[1]
+    peers = lax.axis_size("expert")
+    data_devices = lax.axis_size("dp")
+    line = peers // PAIR
+    units = expert_gate.shape[2]
+    group = peers * tok_count
+    quarter = width // data_devices
+    loss_scale = top_count / math.sqrt(group * data_devices * top_count / experts)
+    vmem = pl.BlockSpec(memory_space=pltpu.VMEM)
+    hbm = pl.BlockSpec(memory_space=pl.ANY)
+    flops = 2 * group * width * (3 * teacher_gate.shape[1] + 7 * units)
+    wide = (quarter, units)
+    tall = (units, quarter)
+    dma = pltpu.SemaphoreType.DMA
+    return pl.pallas_call(
+        functools.partial(fused_kernel, line, data_devices, loss_scale),
+        out_shape=(
+            jax.ShapeDtypeStruct((1,) + wide, F32),
+            jax.ShapeDtypeStruct((1,) + wide, F32),
+            jax.ShapeDtypeStruct((1,) + tall, F32),
+        ),
+        in_specs=[vmem] * 3 + [hbm] * 6,
+        out_specs=(vmem, vmem, vmem),
+        scratch_shapes=[
+            pltpu.VMEM(teacher_gate.shape, BF16),
+            pltpu.VMEM(teacher_up.shape, BF16),
+            pltpu.VMEM(teacher_down.shape, BF16),
+            pltpu.VMEM(expert_gate.shape[1:], BF16),
+            pltpu.VMEM(expert_up.shape[1:], BF16),
+            pltpu.VMEM(expert_down.shape[1:], BF16),
+            pltpu.VMEM((group, width), BF16),
+            pltpu.VMEM((group, width), BF16),
+            pltpu.VMEM((peers, experts, tok_count), F32),
+            pltpu.VMEM((group, units), F32),
+            pltpu.VMEM((group, units), F32),
+            pltpu.VMEM((group, units), BF16),
+            pltpu.VMEM((group, units), BF16),
+            pltpu.VMEM((group, units), BF16),
+            pltpu.VMEM((group, width), BF16),
+            pltpu.VMEM((line, tok_count, width), F32),
+            pltpu.VMEM((line, tok_count, width), BF16),
+            pltpu.VMEM((line, tok_count, width), BF16),
+            pltpu.VMEM((line, tok_count, width), BF16),
+            pltpu.VMEM((2, line, tok_count, width), BF16),
+            pltpu.VMEM((2, PAIR) + wide, BF16),
+            pltpu.VMEM((2, PAIR) + wide, BF16),
+            pltpu.VMEM((PAIR,) + tall, BF16),
+            pltpu.VMEM((PAIR,) + tall, BF16),
+            pltpu.VMEM((2,) + wide, F32),
+            pltpu.VMEM(tall, F32),
+            pltpu.VMEM((2,) + wide, BF16),
+            pltpu.VMEM((2,) + wide, BF16),
+            pltpu.VMEM(tall, BF16),
+            pltpu.VMEM(tall, BF16),
+            dma((6,)),
+            dma((peers - 1,)),
+            dma((peers - 1,)),
+            dma((2, peers)),
+            dma((2, line)),
+            dma((2, line + 1)),
+            dma((line,)),
+            dma((line,)),
+            dma((line,)),
+            dma((2, line)),
+            dma((3, PAIR)),
+            dma((3, PAIR)),
+            dma((3,)),
+            dma((3,)),
+        ],
+        compiler_params=pltpu.CompilerParams(
+            collective_id=0, has_side_effects=True, vmem_limit_bytes=58 * 1024 * 1024
+        ),
+        cost_estimate=pl.CostEstimate(
+            flops=flops, bytes_accessed=8 * width * units, transcendentals=2 * group * units
+        ),
+    )(
+        tokens,
+        router,
+        expert_lists,
+        teacher_gate,
+        teacher_up,
+        teacher_down,
+        expert_gate,
+        expert_up,
+        expert_down,
+    )
+
+
+def fits_kernel(mesh):
+    return mesh.shape["dp"] == PAIR * PAIR and mesh.shape["expert"] <= 4 * PAIR
+
+
 def solution(mesh):
     return jax.shard_map(
-        on_device,
+        fused_on_device if fits_kernel(mesh) else on_device,
         mesh=mesh,
         in_specs=(
             P(("dp", "expert"), None),

time: 310 us -> 153 us (0.49)
  Pallas kernels: 0 us -> 138 us
  waiting for transfers between devices: 125 us -> 0 us
  blocking collectives: 88.2 us -> 0 us
  matrix products: 29.1 us -> 0 us
  local copies, waits for them, and re-layouts: 36.5 us -> 14.2 us
  between operations: 14.1 us -> 0.67 us
  other arithmetic: 13.3 us -> 0 us
  starting transfers between devices: 3.92 us -> 0 us
    pallas_call x0 -> x1, Pallas kernels: none -> 138 us  [fused_on_device(): pl.pallas_call(functools.partial(fused_kernel, line, data_devices, loss_s...]
    reduce_scatter x4 -> x0, waiting for transfers between devices: 90.3 us -> none  [the longest x1 28.1 us: on_device(): lax.psum_scatter(part_gate.astype(jnp.bfloat16), 'dp', scatter_dimension=...]
    all_gather x2 -> x0, blocking collectives: 54.5 us -> none  [the longest x1 28.1 us: on_device(): lax.all_gather(slot_positions, 'expert', axis=0, tiled=True)]
    all_to_all x1 -> x0, blocking collectives: 33.7 us -> none  [on_device(): lax.all_to_all(cot_send, 'expert', split_axis=0, concat_axis=0, tiled=True)]
    all_to_all x1 -> x0, waiting for transfers between devices: 33.5 us -> none  [send_back(): lax.all_to_all(output_blocks, 'expert', split_axis=0, concat_axis=0, tile...]
    dot_general x10 -> x0, matrix products: 29.1 us -> none  [the longest x1 5.17 us: teacher_rows(): jnp.dot(hidden_block, teacher_down, preferred_element_type=jnp.float32)]
    scatter x2 -> x0, local copies, waits for them, and re-layouts: 18.1 us -> none  [the longest x1 15.5 us: on_device(): owner_index = jnp.zeros((expert_devices * capacity,), jnp.int32).at[local...]
    gather x3 -> x0, local copies, waits for them, and re-layouts: 9.72 us -> none  [the longest x1 3.46 us: on_device(): cotangent[entry_row]]
  transfers between devices with their start and end apart: 6 -> 0, of which waited for: 5 -> 0; matrix products, arithmetic and copies ran while one was open for 17% -> 0% of each run, Pallas kernels for 0% -> 0%
where the time goes in v1:
time: 153 us
  Pallas kernels  138 us (90%)
  local copies, waits for them, and re-layouts  14.2 us (9%)
    pallas_call x1, Pallas kernels, fused_on_device(): pl.pallas_call(functools.partial(fused_kernel, line, data_devices, loss_s...  138 us
    unnamed x17, local copies, waits for them, and re-layouts  10.8 us
    pallas_call x2, local copies, waits for them, and re-layouts, fused_on_device(): pl.pallas_call(functools.partial(fused_kernel, line, data_devices, loss_s...  3.47 us

profile of v1, /device:TPU:0, one launch (start us, length us, event | category | flops | bytes accessed | tf_op | source)
XLA Modules:
  0.0 153.0 jit_solution(9186449668149736380)
XLA Ops:
  0.6 0.0 copy-start.4
  0.6 1.5 copy.13.lists_ref
  2.1 1.8 %copy.12.router_ref = f32[1024,8]{1,0:T(8,128)} copy(f32[1024,8]{0,1:T(8,128)} %param.11) | data formatting | bytes 65536 | tf_op args[1]
  3.9 0.0 copy-start
  3.9 2.4 %copy.14.tgate_hbm = bf16[1024,344]{1,0:T(8,128)(2,1)} copy(bf16[1024,344]{0,1:T(8,128)(2,1)} %param.13) | data formatting | bytes 1409024 | tf_op args[4]
  6.2 0.0 copy-done.4
  6.2 1.2 copy.15.tup_hbm
  7.4 0.0 copy-done
  7.4 0.0 copy-start.1
  7.4 1.6 %copy.16.gate_hbm = bf16[1,1024,704]{2,1,0:T(8,128)(2,1)} copy(bf16[1,1024,704]{1,2,0:T(8,128)(2,1)S(1)} %copy-done) | data formatting | bytes 2883584 | tf_op args[7]
  9.0 0.0 copy-done.1
  9.0 1.6 %copy.17.up_hbm = bf16[1,1024,704]{2,1,0:T(8,128)(2,1)} copy(bf16[1,1024,704]{1,2,0:T(8,128)(2,1)S(1)} %copy-done.1) | data formatting | bytes 2883584 | tf_op args[8]
  10.5 138.1 %shard_map.112 = (f32[1,256,704]{2,1,0:T(8,128)}, f32[1,256,704]{2,1,0:T(8,128)}, f32[1,704,256]{2,1,0:T(8,128)}) custom-call(bf16[128,1024]{1,0:T(8,128)(2,1)} %tokens_ref.1, f32[1024,8]{1,0:T(8,128)} %copy.12.router_ref, s32[128,4]{1,0:T(8,128)} %copy.13.lists_ref, bf16[1024,344]{1,0:T(8,128)(2,1)} %copy.14.tgate_hbm, bf16[1024,344]{1,0:T(8,128)(2,1)} %copy.15.tup_hbm, ...), custom_call_target="tpu_custom_call" | custom-call | flops 12499025920 | bytes 5767168 | tf_op jit(solution)/shard_map/pallas_call | solution.py:586
  148.6 0.0 copy-start.2
  148.6 0.0 copy-start.3
  148.6 2.4 %copy.18 = f32[1,256,704]{1,2,0:T(8,128)} copy(f32[1,256,704]{2,1,0:T(8,128)} %get-tuple-element.3) | data formatting | bytes 1441792 | tf_op jit(solution)/shard_map/pallas_call | solution.py:586
  151.0 0.0 copy-done.2
  151.0 1.1 copy.19
  152.1 0.0 copy-done.3
  152.1 0.9 copy.21
Async XLA Ops:
  0.6 5.6 %copy-start.4 = (bf16[1024,344]{0,1:T(8,128)(2,1)S(1)}, bf16[1024,344]{0,1:T(8,128)(2,1)}, u32[]{:S(2)}) copy-start(bf16[1024,344]{0,1:T(8,128)(2,1)} %param.14) | copy-start | bytes 2113540
  3.9 3.5 %copy-start = (bf16[1,1024,704]{1,2,0:T(8,128)(2,1)S(1)}, bf16[1,1024,704]{1,2,0:T(8,128)(2,1)}, u32[]{:S(2)}) copy-start(bf16[1,1024,704]{1,2,0:T(8,128)(2,1)} %param.16) | copy-start | bytes 4325380
  7.4 1.6 %copy-start.1 = (bf16[1,1024,704]{1,2,0:T(8,128)(2,1)S(1)}, bf16[1,1024,704]{1,2,0:T(8,128)(2,1)}, u32[]{:S(2)}) copy-start(bf16[1,1024,704]{1,2,0:T(8,128)(2,1)} %param.17) | copy-start | bytes 4325380
  148.6 2.4 %copy-start.2 = (f32[1,256,704]{2,1,0:T(8,128)S(1)}, f32[1,256,704]{2,1,0:T(8,128)}, u32[]{:S(2)}) copy-start(f32[1,256,704]{2,1,0:T(8,128)} %get-tuple-element.4) | copy-start | bytes 2162692
  148.6 3.5 %copy-start.3 = (f32[1,704,256]{2,1,0:T(8,128)S(1)}, f32[1,704,256]{2,1,0:T(8,128)}, u32[]{:S(2)}) copy-start(f32[1,704,256]{2,1,0:T(8,128)} %get-tuple-element.11) | copy-start | bytes 2162692

commit v2 on v1

--- a/solution.py
+++ b/solution.py
@@ -155,6 +155,7 @@
 
 
 PAIR = 2
+ROW_BY_ROW = (((1,), (1,)), ((), ()))
 BF16 = jnp.bfloat16
 F32 = jnp.float32
 
@@ -185,6 +186,8 @@
     egate,
     eup,
     edown,
+    tdown_turned,
+    edown_turned,
     rows_buf,
     err_buf,
     w_buf,
@@ -201,14 +204,9 @@
     z_recv,
     core_send,
     core_recv,
-    core_send_d,
-    core_recv_d,
     keep,
-    keep_d,
     x_send,
     x_recv,
-    x_send_d,
-    x_recv_d,
     load_sem,
     w_ssem,
     w_rsem,
@@ -225,7 +223,7 @@
     x_rsem,
 ):
     tok_count, width = tokens_ref.shape
-    experts = router_ref.shape[1]
+    experts = router_ref.shape[0]
     dp = lax.axis_index("dp")
     me = lax.axis_index("expert")
     z = me // PAIR
@@ -284,6 +282,8 @@
         load.start()
 
     def block_of(buf, block):
+        if len(buf.shape) == 3:
+            return buf.at[block]
         return buf.at[pl.ds(pl.multiple_of(block * tok_count, tok_count), tok_count)]
 
     block_of(rows_buf, me)[...] = tokens_ref[...]
@@ -326,9 +326,8 @@
                     ).start()
 
                 remote(at, at, ag_ysem.at[turn, d], ag_rsem.at[turn, block], y_peer).start()
-            before = order(step - 1)
-            recv(before * PAIR + 1 - y)
-            work(before)
+            recv(order(step - 1) * PAIR + 1 - y)
+            work(step - 1)
 
     def gather_drain(buf, turn):
         mine = block_of(buf, me)
@@ -358,20 +357,19 @@
 
     gather_start(rows_buf, 0)
 
-    logits = jnp.dot(
+    logits = lax.dot_general(
+        router_ref[...],
         tokens_ref[...].astype(F32),
-        router_ref[...],
+        ROW_BY_ROW,
         precision=lax.Precision.HIGHEST,
         preferred_element_type=F32,
     )
-    expert_ids = lax.broadcasted_iota(jnp.int32, (tok_count, experts), 1)
-    lists = lists_ref[...]
-    chosen = lists[:, 0:1] == expert_ids
-    for k in range(1, lists.shape[1]):
-        chosen = jnp.logical_or(chosen, lists[:, k : k + 1] == expert_ids)
+    expert_ids = lax.broadcasted_iota(jnp.int32, (experts, tok_count), 0)
+    chosen = lists_ref[0:1, :] == expert_ids
+    for k in range(1, lists_ref.shape[0]):
+        chosen = jnp.logical_or(chosen, lists_ref[k : k + 1, :] == expert_ids)
     picked = jnp.where(chosen, jax.nn.sigmoid(logits), 0.0)
-    weights = picked / jnp.sum(picked, axis=1, keepdims=True)
-    w_buf[me] = weights.T
+    w_buf[me] = picked / jnp.sum(picked, axis=0, keepdims=True)
     w_copies = []
     for step in range(1, peers):
         copy = remote(
@@ -385,17 +383,15 @@
         w_copies.append(copy)
     for load in loads:
         load.wait()
+    edown_turned[...] = edown[...].T
+    tdown_turned[...] = tdown[...].T
     for copy in w_copies:
         copy.wait()
 
     def pair_weights(d):
-        columns = []
-        for part in range(PAIR):
-            table_part = w_buf[d * PAIR + part].T
-            columns.append(
-                jnp.sum(jnp.where(expert_ids == me, table_part, 0.0), axis=1, keepdims=True)
-            )
-        return jnp.concatenate(columns, axis=0)
+        return jnp.concatenate(
+            [w_buf[d * PAIR + part, pl.ds(me, 1), :] for part in range(PAIR)], axis=1
+        )
 
     def pair_of(d):
         return pl.ds(pl.multiple_of(d * pair_rows, pair_rows), pair_rows)
@@ -405,64 +401,61 @@
             y_send.at[d], y_recv.at[d], rs_ysem.at[d], rs_yrsem.at[d], y_peer
         )
 
-    def forward(d):
+    def z_copy(d):
+        return remote(
+            z_send.at[d],
+            z_recv.at[z],
+            rs_zsem.at[d],
+            rs_zrsem.at[z],
+            (dp, d * PAIR + y),
+        )
+
+    def forward(step):
+        d = order(step)
         where = pair_of(d)
         rows = rows_buf[where, :]
-        pre_a = jnp.dot(rows, tgate[...], preferred_element_type=F32)
-        pre_b = jnp.dot(rows, tup[...], preferred_element_type=F32)
-        teacher_hidden = (silu_value(pre_a) * pre_b).astype(BF16)
-        teacher = jnp.dot(teacher_hidden, tdown[...], preferred_element_type=F32)
-        gate_values = jnp.dot(rows, egate[...], preferred_element_type=F32)
-        up_values = jnp.dot(rows, eup[...], preferred_element_type=F32)
-        pre_gate[where, :] = gate_values
-        pre_up[where, :] = up_values
+
+        def product(table):
+            return lax.dot_general(table[...], rows, ROW_BY_ROW, preferred_element_type=F32)
+
+        gate_values = product(egate)
+        up_values = product(eup)
+        pre_gate[:, where] = gate_values
+        pre_up[:, where] = up_values
         hidden_values = (silu_value(gate_values) * up_values).astype(BF16)
-        hidden[where, :] = hidden_values
-        output = jnp.dot(hidden_values, edown[...], preferred_element_type=F32)
+        hidden[:, where] = hidden_values
+        teacher_hidden = (silu_value(product(tgate)) * product(tup)).astype(BF16)
+        output = jnp.dot(edown_turned[...], hidden_values, preferred_element_type=F32)
+        teacher = jnp.dot(tdown_turned[...], teacher_hidden, preferred_element_type=F32)
         partial = pair_weights(d) * output - teacher
-        low = partial[:tok_count]
-        high = partial[tok_count:]
-        part_own[d] = jnp.where(y == 0, low, high)
+        low = partial[:, :tok_count]
+        high = partial[:, tok_count:]
         y_send[d] = jnp.where(y == 0, high, low).astype(BF16)
         y_copy(d).start()
-
-    gather_rest(rows_buf, 0, forward)
-
-    def z_copy(d):
-        rising = d > z
-        way = jnp.where(rising, 0, 1)
-        return remote(
-            z_send.at[d],
-            z_recv.at[way, d],
-            rs_zsem.at[d],
-            rs_zrsem.at[way, d],
-            (dp, jnp.where(rising, me + PAIR, me - PAIR)),
-        )
-
-    def z_arrived(way, d):
-        remote(
-            z_send.at[d], z_recv.at[way, d], rs_zsem.at[d], rs_zrsem.at[way, d], y_peer
-        ).wait_recv()
-        part_own[d] += z_recv[way, d].astype(F32)
-
-    for step in range(line - 1, -1, -1):
+        part_own[d] = jnp.where(y == 0, low, high)
+        if step > 1:
+            combine(step - 1)
+
+    def combine(step):
         d = order(step)
         y_copy(d).wait_recv()
-        part_own[d] += y_recv[d].astype(F32)
-
-        @pl.when(jnp.logical_and(d >= z, z > 0))
-        def _():
-            z_arrived(0, d)
-
-        @pl.when(jnp.logical_and(d <= z, z < line - 1))
-        def _():
-            z_arrived(1, d)
-
+        total = part_own[d] + y_recv[d].astype(F32)
         if step:
-            z_send[d] = part_own[d].astype(BF16)
+            z_send[d] = total.astype(BF16)
             z_copy(d).start()
         else:
-            block_of(err_buf, me)[...] = (part_own[d] * loss_scale).astype(BF16)
+            part_own[d] = total
+
+    gather_rest(rows_buf, 0, forward)
+    combine(line - 1)
+    combine(0)
+    for step in range(1, line):
+        d = order(step)
+        remote(
+            z_send.at[d], z_recv.at[d], rs_zsem.at[d], rs_zrsem.at[d], y_peer
+        ).wait_recv()
+        part_own[z] += z_recv[d].astype(F32)
+    err_buf[me] = (part_own[z] * loss_scale).astype(BF16)
 
     gather_start(err_buf, 1)
     gather_drain(rows_buf, 0)
@@ -472,46 +465,40 @@
         if step:
             z_copy(d).wait_send()
 
-    def backward(d):
+    def backward(step):
+        d = order(step)
         where = pair_of(d)
-        cot_values = (pair_weights(d) * err_buf[where, :].astype(F32)).astype(BF16)
-        cot[where, :] = cot_values
-        grad_hidden = lax.dot_general(
-            cot_values, edown[...], (((1,), (1,)), ((), ())), preferred_element_type=F32
-        )
-        gate_values = pre_gate[where, :]
+        errors = jnp.concatenate([err_buf[d * PAIR + part] for part in range(PAIR)], axis=1)
+        cot_values = (pair_weights(d) * errors.astype(F32)).astype(BF16)
+        cot[:, where] = cot_values
+        grad_hidden = jnp.dot(edown[...], cot_values, preferred_element_type=F32)
+        gate_values = pre_gate[:, where]
         gate_sigmoid = jax.nn.sigmoid(gate_values)
-        grad_pre_gate[where, :] = (
+        grad_pre_gate[:, where] = (
             grad_hidden
-            * pre_up[where, :]
+            * pre_up[:, where]
             * gate_sigmoid
             * (1.0 + gate_values * (1.0 - gate_sigmoid))
         ).astype(BF16)
-        grad_pre_up[where, :] = (grad_hidden * (gate_values * gate_sigmoid)).astype(BF16)
+        grad_pre_up[:, where] = (grad_hidden * (gate_values * gate_sigmoid)).astype(BF16)
 
     gather_rest(err_buf, 1, backward)
 
     quarter = width // data_devices
-    contract = (((0,), (0,)), ((), ()))
 
     def part(which, q):
         columns = pl.ds(pl.multiple_of(q * quarter, quarter), quarter)
         if which == 2:
             return lax.dot_general(
-                hidden[...], cot[:, columns], contract, preferred_element_type=F32
+                hidden[...], cot[columns, :], ROW_BY_ROW, preferred_element_type=F32
             )
         grads = grad_pre_gate if which == 0 else grad_pre_up
-        return lax.dot_general(
-            rows_buf[:, columns], grads[...], contract, preferred_element_type=F32
-        )
-
-    def at_part(which, wide, tall):
-        return tall if which == 2 else wide.at[which]
+        return jnp.dot(grads[...], rows_buf[:, columns], preferred_element_type=F32)
 
     def core_copy(which, slot):
         return remote(
-            at_part(which, core_send, core_send_d).at[slot],
-            at_part(which, core_recv, core_recv_d).at[slot],
+            core_send.at[which, slot],
+            core_recv.at[which, slot],
             c_ssem.at[which, slot],
             c_rsem.at[which, slot],
             core_peer,
@@ -519,37 +506,37 @@
 
     def x_copy(which):
         return remote(
-            at_part(which, x_send, x_send_d),
-            at_part(which, x_recv, x_recv_d),
+            x_send.at[which],
+            x_recv.at[which],
             x_ssem.at[which],
             x_rsem.at[which],
             x_peer,
         )
 
     x_of = (1 - x_at, x_at)
-    for which in (0, 1, 2):
-        held = at_part(which, keep, keep_d)
-        sends = at_part(which, core_send, core_send_d)
-        recvs = at_part(which, core_recv, core_recv_d)
-        for slot in range(PAIR):
-            sends[slot] = part(which, x_of[slot] * PAIR + 1 - core).astype(BF16)
-            core_copy(which, slot).start()
-            own = part(which, x_of[slot] * PAIR + core)
-            core_copy(which, slot).wait_recv()
-            total = own + recvs[slot].astype(F32)
-            if slot == 0:
-                at_part(which, x_send, x_send_d)[...] = total.astype(BF16)
-                x_copy(which).start()
-            else:
-                held[...] = total
-    outs = (out_gate, out_up, out_down)
-    for which in (0, 1, 2):
+
+    def join(which, slot):
+        core_copy(which, slot).wait_recv()
+        total = keep[which, slot] + core_recv[which, slot].astype(F32)
+        if slot == 0:
+            x_send[which] = total.astype(BF16)
+            x_copy(which).start()
+        else:
+            keep[which, slot] = total
+
+    items = [(which, slot) for slot in range(PAIR) for which in range(3)]
+    for at, (which, slot) in enumerate(items):
+        core_send[which, slot] = part(which, x_of[slot] * PAIR + 1 - core).astype(BF16)
+        core_copy(which, slot).start()
+        keep[which, slot] = part(which, x_of[slot] * PAIR + core)
+        if at:
+            join(*items[at - 1])
+    join(*items[-1])
+    for which, out in enumerate((out_gate, out_up, out_down)):
         x_copy(which).wait_recv()
-        outs[which][0] = (
-            at_part(which, keep, keep_d)[...] + at_part(which, x_recv, x_recv_d)[...].astype(F32)
-        )
+        out[0] = keep[which, 1] + x_recv[which].astype(F32)
     gather_drain(err_buf, 1)
-    for which in (0, 1, 2):
+    for which in range(3):
         x_copy(which).wait_send()
         for slot in range(PAIR):
             core_copy(which, slot).wait_send()
@@ -580,49 +567,41 @@
     vmem = pl.BlockSpec(memory_space=pltpu.VMEM)
     hbm = pl.BlockSpec(memory_space=pl.ANY)
     flops = 2 * group * width * (3 * teacher_gate.shape[1] + 7 * units)
-    wide = (quarter, units)
     tall = (units, quarter)
     dma = pltpu.SemaphoreType.DMA
-    return pl.pallas_call(
+    grad_gate, grad_up, grad_down = pl.pallas_call(
         functools.partial(fused_kernel, line, data_devices, loss_scale),
-        out_shape=(
-            jax.ShapeDtypeStruct((1,) + wide, F32),
-            jax.ShapeDtypeStruct((1,) + wide, F32),
-            jax.ShapeDtypeStruct((1,) + tall, F32),
-        ),
+        out_shape=(jax.ShapeDtypeStruct((1,) + tall, F32),) * 3,
         in_specs=[vmem] * 3 + [hbm] * 6,
-        out_specs=(vmem, vmem, vmem),
+        out_specs=(vmem,) * 3,
         scratch_shapes=[
-            pltpu.VMEM(teacher_gate.shape, BF16),
-            pltpu.VMEM(teacher_up.shape, BF16),
+            pltpu.VMEM(teacher_gate.shape[::-1], BF16),
+            pltpu.VMEM(teacher_up.shape[::-1], BF16),
             pltpu.VMEM(teacher_down.shape, BF16),
-            pltpu.VMEM(expert_gate.shape[1:], BF16),
-            pltpu.VMEM(expert_up.shape[1:], BF16),
-            pltpu.VMEM(expert_down.shape[1:], BF16),
+            pltpu.VMEM((units, width), BF16),
+            pltpu.VMEM((units, width), BF16),
+            pltpu.VMEM((units, width), BF16),
+            pltpu.VMEM(teacher_down.shape[::-1], BF16),
+            pltpu.VMEM((width, units), BF16),
             pltpu.VMEM((group, width), BF16),
-            pltpu.VMEM((group, width), BF16),
+            pltpu.VMEM((peers, width, tok_count), BF16),
             pltpu.VMEM((peers, experts, tok_count), F32),
-            pltpu.VMEM((group, units), F32),
-            pltpu.VMEM((group, units), F32),
-            pltpu.VMEM((group, units), BF16),
-            pltpu.VMEM((group, units), BF16),
-            pltpu.VMEM((group, units), BF16),
-            pltpu.VMEM((group, width), BF16),
-            pltpu.VMEM((line, tok_count, width), F32),
-            pltpu.VMEM((line, tok_count, width), BF16),
-            pltpu.VMEM((line, tok_count, width), BF16),
-            pltpu.VMEM((line, tok_count, width), BF16),
-            pltpu.VMEM((2, line, tok_count, width), BF16),
-            pltpu.VMEM((2, PAIR) + wide, BF16),
-            pltpu.VMEM((2, PAIR) + wide, BF16),
-            pltpu.VMEM((PAIR,) + tall, BF16),
-            pltpu.VMEM((PAIR,) + tall, BF16),
-            pltpu.VMEM((2,) + wide, F32),
-            pltpu.VMEM(tall, F32),
-            pltpu.VMEM((2,) + wide, BF16),
-            pltpu.VMEM((2,) + wide, BF16),
-            pltpu.VMEM(tall, BF16),
-            pltpu.VMEM(tall, BF16),
+            pltpu.VMEM((units, group), F32),
+            pltpu.VMEM((units, group), F32),
+            pltpu.VMEM((units, group), BF16),
+            pltpu.VMEM((units, group), BF16),
+            pltpu.VMEM((units, group), BF16),
+            pltpu.VMEM((width, group), BF16),
+            pltpu.VMEM((line, width, tok_count), F32),
+            pltpu.VMEM((line, width, tok_count), BF16),
+            pltpu.VMEM((line, width, tok_count), BF16),
+            pltpu.VMEM((line, width, tok_count), BF16),
+            pltpu.VMEM((line, width, tok_count), BF16),
+            pltpu.VMEM((3, PAIR) + tall, BF16),
+            pltpu.VMEM((3, PAIR) + tall, BF16),
+            pltpu.VMEM((3, PAIR) + tall, F32),
+            pltpu.VMEM((3,) + tall, BF16),
+            pltpu.VMEM((3,) + tall, BF16),
             dma((6,)),
             dma((peers - 1,)),
             dma((peers - 1,)),
@@ -632,7 +611,7 @@
             dma((line,)),
             dma((line,)),
             dma((line,)),
-            dma((2, line)),
+            dma((line,)),
             dma((3, PAIR)),
             dma((3, PAIR)),
             dma((3,)),
@@ -646,15 +625,16 @@
         ),
     )(
         tokens,
-        router,
-        expert_lists,
-        teacher_gate,
-        teacher_up,
+        router.T,
+        expert_lists.T,
+        teacher_gate.T,
+        teacher_up.T,
         teacher_down,
-        expert_gate,
-        expert_up,
+        jnp.swapaxes(expert_gate, 1, 2),
+        jnp.swapaxes(expert_up, 1, 2),
         expert_down,
     )
+    return (jnp.swapaxes(grad_gate, 1, 2), jnp.swapaxes(grad_up, 1, 2), grad_down)
 
 
 def fits_kernel(mesh):

time: 153 us -> 131 us (0.86)
  Pallas kernels: 138 us -> 126 us
  local copies, waits for them, and re-layouts: 14.2 us -> 3.85 us
    pallas_call x1, Pallas kernels: 138 us -> 126 us  [fused_on_device(): pl.pallas_call(functools.partial(fused_kernel, line, data_devices, loss_s...]
    unnamed x17 -> x7, local copies, waits for them, and re-layouts: 10.8 us -> 3.85 us
    pallas_call x2 -> x0, local copies, waits for them, and re-layouts: 3.47 us -> none  [fused_on_device(): pl.pallas_call(functools.partial(fused_kernel, line, data_devices, loss_s...]
where the time goes in v2:
time: 131 us; the launch traced here: 130 us
  Pallas kernels  126 us (96%)
  local copies, waits for them, and re-layouts  3.85 us (3%)
    pallas_call x1, Pallas kernels, fused_on_device(): pl.pallas_call(functools.partial(fused_kernel, line, data_devices, loss_s...  126 us
    unnamed x7, local copies, waits for them, and re-layouts  3.85 us

profile of v2, /device:TPU:0, one launch (start us, length us, event | category | flops | bytes accessed | tf_op | source)
XLA Modules:
  0.0 130.5 jit_solution(164908904519873200)
XLA Ops:
  0.6 126.0 %shard_map.112 = (f32[1,704,256]{2,1,0:T(8,128)}, f32[1,704,256]{2,1,0:T(8,128)}, f32[1,704,256]{2,1,0:T(8,128)}) custom-call(bf16[128,1024]{1,0:T(8,128)(2,1)} %tokens_ref.1, f32[8,1024]{1,0:T(8,128)} %bitcast.14, s32[4,128]{1,0:T(4,128)} %bitcast.15, bf16[344,1024]{1,0:T(8,128)(2,1)} %bitcast.12, bf16[344,1024]{1,0:T(8,128)(2,1)} %bitcast.13, ...), custom_call_target="tpu_custom_call" | custom-call | flops 12499025920 | bytes 5767168 | tf_op jit(solution)/shard_map/pallas_call | solution.py:572
  126.6 0.0 copy-start.1
  126.6 0.0 copy-start
  126.6 2.1 %copy.15 = f32[1,256,704]{1,2,0:T(8,128)} copy(f32[1,256,704]{1,2,0:T(8,128)} %bitcast.9) | data formatting | bytes 1441792
  128.7 0.0 copy-done.1
  128.7 0.9 copy.16
  129.6 0.0 copy-done
  129.6 0.9 copy.17
Async XLA Ops:
  126.6 2.1 %copy-start.1 = (f32[1,704,256]{2,1,0:T(8,128)S(1)}, f32[1,704,256]{2,1,0:T(8,128)}, u32[]{:S(2)}) copy-start(f32[1,704,256]{2,1,0:T(8,128)} %get-tuple-element.7) | copy-start | bytes 2162692
  126.6 3.0 %copy-start = (f32[1,704,256]{2,1,0:T(8,128)S(1)}, f32[1,704,256]{2,1,0:T(8,128)}, u32[]{:S(2)}) copy-start(f32[1,704,256]{2,1,0:T(8,128)} %get-tuple-element.14) | copy-start | bytes 2162692

commit v3 on v2

--- a/solution.py
+++ b/solution.py
@@ -155,6 +155,7 @@
 
 
 PAIR = 2
+PIECES = 2
 ROW_BY_ROW = (((1,), (1,)), ((), ()))
 BF16 = jnp.bfloat16
 F32 = jnp.float32
@@ -281,81 +282,107 @@
     for load in loads:
         load.start()
 
-    def block_of(buf, block):
+    def piece_of(buf, block, piece):
         if len(buf.shape) == 3:
-            return buf.at[block]
-        return buf.at[pl.ds(pl.multiple_of(block * tok_count, tok_count), tok_count)]
-
-    block_of(rows_buf, me)[...] = tokens_ref[...]
+            span = buf.shape[1] // PIECES
+            return buf.at[block, pl.ds(piece * span, span)]
+        span = tok_count // PIECES
+        first = pl.multiple_of(block * tok_count + piece * span, span)
+        return buf.at[pl.ds(first, span)]
+
+    rows_buf[pl.ds(pl.multiple_of(me * tok_count, tok_count), tok_count), :] = tokens_ref[...]
     pl.semaphore_wait(barrier, peers - 1 + 2)
 
-    def gather_start(buf, turn):
-        mine = block_of(buf, me)
+    def own_copies(buf, turn, piece):
+        mine = piece_of(buf, me, piece)
+        arrival = ag_rsem.at[turn, me, piece]
+        sent = ag_zsem.at[turn]
+        return (
+            remote(mine, mine, ag_ysem.at[turn, z, piece], arrival, y_peer),
+            remote(mine, mine, sent.at[z, piece], arrival, (dp, me + PAIR)),
+            remote(mine, mine, sent.at[line, piece], arrival, (dp, me - PAIR)),
+        )
+
+    def gather_start(buf, turn, piece):
+        across, rising, falling = own_copies(buf, turn, piece)
 
         @pl.when(z < line - 1)
         def _():
-            remote(mine, mine, ag_zsem.at[turn, z], ag_rsem.at[turn, me], (dp, me + PAIR)).start()
+            rising.start()
 
         @pl.when(z > 0)
         def _():
-            remote(mine, mine, ag_zsem.at[turn, line], ag_rsem.at[turn, me], (dp, me - PAIR)).start()
-
-        remote(mine, mine, ag_ysem.at[turn, z], ag_rsem.at[turn, me], y_peer).start()
-
-    def away(d):
-        onward = jnp.where(d < z, z < line - 1, z > 0)
-        return onward, (dp, jnp.where(d < z, me + PAIR, me - PAIR))
+            falling.start()
+
+        across.start()
+
+    def onward_copies(buf, turn, d, piece):
+        block = d * PAIR + y
+        at = piece_of(buf, block, piece)
+        arrival = ag_rsem.at[turn, block, piece]
+        device = (dp, jnp.where(d < z, me + PAIR, me - PAIR))
+        return (
+            remote(at, at, ag_ysem.at[turn, d, piece], arrival, y_peer),
+            remote(at, at, ag_zsem.at[turn, d, piece], arrival, device),
+            jnp.where(d < z, z < line - 1, z > 0),
+        )
 
     def gather_rest(buf, turn, work):
-        def recv(block):
-            at = block_of(buf, block)
-            remote(at, at, ag_ysem.at[turn, 0], ag_rsem.at[turn, block], y_peer).wait_recv()
-
-        for step in range(1, line + 1):
-            if step < line:
-                d = order(step)
-                block = d * PAIR + y
-                recv(block)
-                at = block_of(buf, block)
-                onward, device = away(d)
+        def recv(block, piece):
+            at = piece_of(buf, block, piece)
+            remote(
+                at, at, ag_ysem.at[turn, 0, piece], ag_rsem.at[turn, block, piece], y_peer
+            ).wait_recv()
+
+        def do_work(step):
+            for piece in range(PIECES):
+                recv(order(step) * PAIR + 1 - y, piece)
+            work(step)
+
+        done = 0
+        for step in range(1, line):
+            d = order(step)
+            for piece in range(PIECES):
+                recv(d * PAIR + y, piece)
+                across, further, onward = onward_copies(buf, turn, d, piece)
 
                 @pl.when(onward)
                 def _():
-                    remote(
-                        at, at, ag_zsem.at[turn, d], ag_rsem.at[turn, block], device
-                    ).start()
-
-                remote(at, at, ag_ysem.at[turn, d], ag_rsem.at[turn, block], y_peer).start()
-            recv(order(step - 1) * PAIR + 1 - y)
-            work(step - 1)
+                    further.start()
+
+                across.start()
+            if step > 1 or line == 2:
+                while done < step:
+                    do_work(done)
+                    done += 1
+        while done < line:
+            do_work(done)
+            done += 1
 
     def gather_drain(buf, turn):
-        mine = block_of(buf, me)
-
-        @pl.when(z < line - 1)
-        def _():
-            remote(mine, mine, ag_zsem.at[turn, z], ag_rsem.at[turn, me], (dp, me + PAIR)).wait_send()
-
-        @pl.when(z > 0)
-        def _():
-            remote(mine, mine, ag_zsem.at[turn, line], ag_rsem.at[turn, me], (dp, me - PAIR)).wait_send()
-
-        for step in range(line):
-            d = order(step)
-            block = d * PAIR + y
-            at = block_of(buf, block)
-            if step:
-                onward, device = away(d)
+        for piece in range(PIECES):
+            across, rising, falling = own_copies(buf, turn, piece)
+
+            @pl.when(z < line - 1)
+            def _():
+                rising.wait_send()
+
+            @pl.when(z > 0)
+            def _():
+                falling.wait_send()
+
+            across.wait_send()
+            for step in range(1, line):
+                across, further, onward = onward_copies(buf, turn, order(step), piece)
 
                 @pl.when(onward)
                 def _():
-                    remote(
-                        at, at, ag_zsem.at[turn, d], ag_rsem.at[turn, block], device
-                    ).wait_send()
-
-            remote(at, at, ag_ysem.at[turn, d], ag_rsem.at[turn, block], y_peer).wait_send()
-
-    gather_start(rows_buf, 0)
+                    further.wait_send()
+
+                across.wait_send()
+
+    for piece in range(PIECES):
+        gather_start(rows_buf, 0, piece)
 
     logits = lax.dot_general(
         router_ref[...],
@@ -396,17 +423,25 @@
     def pair_of(d):
         return pl.ds(pl.multiple_of(d * pair_rows, pair_rows), pair_rows)
 
-    def y_copy(d):
+    span = width // PIECES
+
+    def y_copy(d, piece):
+        at = (d, pl.ds(piece * span, span))
         return remote(
-            y_send.at[d], y_recv.at[d], rs_ysem.at[d], rs_yrsem.at[d], y_peer
-        )
-
-    def z_copy(d):
+            y_send.at[at],
+            y_recv.at[at],
+            rs_ysem.at[d, piece],
+            rs_yrsem.at[d, piece],
+            y_peer,
+        )
+
+    def z_copy(d, piece):
+        part_rows = pl.ds(piece * span, span)
         return remote(
-            z_send.at[d],
-            z_recv.at[z],
-            rs_zsem.at[d],
-            rs_zrsem.at[z],
+            z_send.at[d, part_rows],
+            z_recv.at[z, part_rows],
+            rs_zsem.at[d, piece],
+            rs_zrsem.at[z, piece],
             (dp, d * PAIR + y),
         )
 
@@ -425,53 +460,69 @@
         hidden_values = (silu_value(gate_values) * up_values).astype(BF16)
         hidden[:, where] = hidden_values
         teacher_hidden = (silu_value(product(tgate)) * product(tup)).astype(BF16)
-        output = jnp.dot(edown_turned[...], hidden_values, preferred_element_type=F32)
-        teacher = jnp.dot(tdown_turned[...], teacher_hidden, preferred_element_type=F32)
-        partial = pair_weights(d) * output - teacher
-        low = partial[:, :tok_count]
-        high = partial[:, tok_count:]
-        y_send[d] = jnp.where(y == 0, high, low).astype(BF16)
-        y_copy(d).start()
-        part_own[d] = jnp.where(y == 0, low, high)
+        scale = pair_weights(d)
+        for piece in range(PIECES):
+            at = pl.ds(piece * span, span)
+            output = jnp.dot(edown_turned[at, :], hidden_values, preferred_element_type=F32)
+            teacher = jnp.dot(tdown_turned[at, :], teacher_hidden, preferred_element_type=F32)
+            partial = scale * output - teacher
+            low = partial[:, :tok_count]
+            high = partial[:, tok_count:]
+            y_send[d, at] = jnp.where(y == 0, high, low).astype(BF16)
+            y_copy(d, piece).start()
+            part_own[d, at] = jnp.where(y == 0, low, high)
         if step > 1:
-            combine(step - 1)
-
-    def combine(step):
+            for piece in range(PIECES):
+                combine(step - 1, piece)
+
+    def combine(step, piece):
         d = order(step)
-        y_copy(d).wait_recv()
-        total = part_own[d] + y_recv[d].astype(F32)
+        at = pl.ds(piece * span, span)
+        y_copy(d, piece).wait_recv()
+        total = part_own[d, at] + y_recv[d, at].astype(F32)
         if step:
-            z_send[d] = total.astype(BF16)
-            z_copy(d).start()
+            z_send[d, at] = total.astype(BF16)
+            z_copy(d, piece).start()
         else:
-            part_own[d] = total
+            part_own[d, at] = total
 
     gather_rest(rows_buf, 0, forward)
-    combine(line - 1)
-    combine(0)
-    for step in range(1, line):
+    for piece in range(PIECES):
+        combine(line - 1, piece)
+    for piece in range(PIECES):
+        combine(0, piece)
+    for piece in range(PIECES):
+        at = pl.ds(piece * span, span)
+        total = part_own[z, at]
+        for step in range(1, line):
+            d = order(step)
+            remote(
+                z_send.at[d, at],
+                z_recv.at[d, at],
+                rs_zsem.at[d, piece],
+                rs_zrsem.at[d, piece],
+                y_peer,
+            ).wait_recv()
+            total += z_recv[d, at].astype(F32)
+        err_buf[me, at] = (total * loss_scale).astype(BF16)
+        gather_start(err_buf, 1, piece)
+
+    gather_drain(rows_buf, 0)
+    for piece in range(PIECES):
+        for step in range(line):
+            d = order(step)
+            y_copy(d, piece).wait_send()
+            if step:
+                z_copy(d, piece).wait_send()
+
+    def cotangents(step):
         d = order(step)
-        remote(
-            z_send.at[d], z_recv.at[d], rs_zsem.at[d], rs_zrsem.at[d], y_peer
-        ).wait_recv()
-        part_own[z] += z_recv[d].astype(F32)
-    err_buf[me] = (part_own[z] * loss_scale).astype(BF16)
-
-    gather_start(err_buf, 1)
-    gather_drain(rows_buf, 0)
-    for step in range(line):
-        d = order(step)
-        y_copy(d).wait_send()
-        if step:
-            z_copy(d).wait_send()
-
-    def backward(step):
-        d = order(step)
-        where = pair_of(d)
         errors = jnp.concatenate([err_buf[d * PAIR + part] for part in range(PAIR)], axis=1)
-        cot_values = (pair_weights(d) * errors.astype(F32)).astype(BF16)
-        cot[:, where] = cot_values
-        grad_hidden = jnp.dot(edown[...], cot_values, preferred_element_type=F32)
+        cot[:, pair_of(d)] = (pair_weights(d) * errors.astype(F32)).astype(BF16)
+
+    def hidden_grads(step):
+        where = pair_of(order(step))
+        grad_hidden = jnp.dot(edown[...], cot[:, where], preferred_element_type=F32)
         gate_values = pre_gate[:, where]
         gate_sigmoid = jax.nn.sigmoid(gate_values)
         grad_pre_gate[:, where] = (
@@ -482,6 +533,11 @@
         ).astype(BF16)
         grad_pre_up[:, where] = (grad_hidden * (gate_values * gate_sigmoid)).astype(BF16)
 
+    def backward(step):
+        cotangents(step)
+        if step < line - 1:
+            hidden_grads(step)
+
     gather_rest(err_buf, 1, backward)
 
     quarter = width // data_devices
@@ -524,11 +580,13 @@
         else:
             keep[which, slot] = total
 
-    items = [(which, slot) for slot in range(PAIR) for which in range(3)]
+    items = [(which, slot) for slot in range(PAIR) for which in (2, 0, 1)]
     for at, (which, slot) in enumerate(items):
         core_send[which, slot] = part(which, x_of[slot] * PAIR + 1 - core).astype(BF16)
         core_copy(which, slot).start()
         keep[which, slot] = part(which, x_of[slot] * PAIR + core)
+        if at == 0:
+            hidden_grads(line - 1)
         if at:
             join(*items[at - 1])
     join(*items[-1])
@@ -605,13 +663,13 @@
             dma((6,)),
             dma((peers - 1,)),
             dma((peers - 1,)),
-            dma((2, peers)),
-            dma((2, line)),
-            dma((2, line + 1)),
-            dma((line,)),
-            dma((line,)),
-            dma((line,)),
-            dma((line,)),
+            dma((2, peers, PIECES)),
+            dma((2, line, PIECES)),
+            dma((2, line + 1, PIECES)),
+            dma((line, PIECES)),
+            dma((line, PIECES)),
+            dma((line, PIECES)),
+            dma((line, PIECES)),
             dma((3, PAIR)),
             dma((3, PAIR)),
             dma((3,)),

time: 131 us -> 124 us (0.947)
  Pallas kernels: 126 us -> 119 us
    pallas_call x1, Pallas kernels: 126 us -> 119 us  [fused_on_device(): pl.pallas_call(functools.partial(fused_kernel, line, data_devices, loss_s...]
where the time goes in v3:
time: 124 us
  Pallas kernels  119 us (96%)
  local copies, waits for them, and re-layouts  3.85 us (3%)
    pallas_call x1, Pallas kernels, fused_on_device(): pl.pallas_call(functools.partial(fused_kernel, line, data_devices, loss_s...  119 us
    unnamed x7, local copies, waits for them, and re-layouts  3.85 us

profile of v3, /device:TPU:0, one launch (start us, length us, event | category | flops | bytes accessed | tf_op | source)
XLA Modules:
  0.0 123.7 jit_solution(661981831295422964)
XLA Ops:
  0.6 119.2 %shard_map.112 = (f32[1,704,256]{2,1,0:T(8,128)}, f32[1,704,256]{2,1,0:T(8,128)}, f32[1,704,256]{2,1,0:T(8,128)}) custom-call(bf16[128,1024]{1,0:T(8,128)(2,1)} %tokens_ref.1, f32[8,1024]{1,0:T(8,128)} %bitcast.14, s32[4,128]{1,0:T(4,128)} %bitcast.15, bf16[344,1024]{1,0:T(8,128)(2,1)} %bitcast.12, bf16[344,1024]{1,0:T(8,128)(2,1)} %bitcast.13, ...), custom_call_target="tpu_custom_call" | custom-call | flops 12499025920 | bytes 5767168 | tf_op jit(solution)/shard_map/pallas_call | solution.py:630
  119.9 0.0 copy-start.1
  119.9 0.0 copy-start
  119.9 2.1 %copy.15 = f32[1,256,704]{1,2,0:T(8,128)} copy(f32[1,256,704]{1,2,0:T(8,128)} %bitcast.9) | data formatting | bytes 1441792
  122.0 0.0 copy-done.1
  122.0 0.9 copy.16
  122.9 0.0 copy-done
  122.9 0.9 copy.17
Async XLA Ops:
  119.9 2.1 %copy-start.1 = (f32[1,704,256]{2,1,0:T(8,128)S(1)}, f32[1,704,256]{2,1,0:T(8,128)}, u32[]{:S(2)}) copy-start(f32[1,704,256]{2,1,0:T(8,128)} %get-tuple-element.7) | copy-start | bytes 2162692
  119.9 3.0 %copy-start = (f32[1,704,256]{2,1,0:T(8,128)S(1)}, f32[1,704,256]{2,1,0:T(8,128)}, u32[]{:S(2)}) copy-start(f32[1,704,256]{2,1,0:T(8,128)} %get-tuple-element.14) | copy-start | bytes 2162692

commit v4 on v3

--- a/solution.py
+++ b/solution.py
@@ -155,7 +155,8 @@
 
 
 PAIR = 2
-PIECES = 2
+PIECES = 4
+Y_FIRST = 1
 ROW_BY_ROW = (((1,), (1,)), ((), ()))
 BF16 = jnp.bfloat16
 F32 = jnp.float32
@@ -206,6 +207,7 @@
     core_send,
     core_recv,
     keep,
+    down_early,
     x_send,
     x_recv,
     load_sem,
@@ -214,6 +216,7 @@
     ag_rsem,
     ag_ysem,
     ag_zsem,
+    ag_osem,
     rs_ysem,
     rs_yrsem,
     rs_zsem,
@@ -327,6 +330,25 @@
             jnp.where(d < z, z < line - 1, z > 0),
         )
 
+    def relay_copies(buf, turn, piece):
+        block = me + 1 - 2 * y
+        at = piece_of(buf, block, piece)
+        arrival = ag_rsem.at[turn, block, piece]
+        sent = ag_osem.at[turn]
+        return (
+            remote(at, at, sent.at[z, piece], arrival, (dp, me + PAIR)),
+            remote(at, at, sent.at[line, piece], arrival, (dp, me - PAIR)),
+        )
+
+    def other_onward(buf, turn, d, piece):
+        block = d * PAIR + 1 - y
+        at = piece_of(buf, block, piece)
+        device = (dp, jnp.where(d < z, me + PAIR, me - PAIR))
+        return (
+            remote(at, at, ag_osem.at[turn, d, piece], ag_rsem.at[turn, block, piece], device),
+            jnp.where(d < z, z < line - 1, z > 0),
+        )
+
     def gather_rest(buf, turn, work):
         def recv(block, piece):
             at = piece_of(buf, block, piece)
@@ -335,9 +357,21 @@
             ).wait_recv()
 
         def do_work(step):
-            for piece in range(PIECES):
+            for piece in range(Y_FIRST, PIECES):
                 recv(order(step) * PAIR + 1 - y, piece)
             work(step)
+
+        for piece in range(Y_FIRST):
+            recv(me + 1 - 2 * y, piece)
+            rising, falling = relay_copies(buf, turn, piece)
+
+            @pl.when(z < line - 1)
+            def _():
+                rising.start()
+
+            @pl.when(z > 0)
+            def _():
+                falling.start()
 
         done = 0
         for step in range(1, line):
@@ -350,7 +384,16 @@
                 def _():
                     further.start()
 
-                across.start()
+                if piece >= Y_FIRST:
+                    across.start()
+            for piece in range(Y_FIRST):
+                recv(d * PAIR + 1 - y, piece)
+                beside, onward = other_onward(buf, turn, d, piece)
+
+                @pl.when(onward)
+                def _():
+                    beside.start()
+
             if step > 1 or line == 2:
                 while done < step:
                     do_work(done)
@@ -379,7 +422,26 @@
                 def _():
                     further.wait_send()
 
-                across.wait_send()
+                if piece >= Y_FIRST:
+                    across.wait_send()
+        for piece in range(Y_FIRST):
+            rising, falling = relay_copies(buf, turn, piece)
+
+            @pl.when(z < line - 1)
+            def _():
+                rising.wait_send()
+
+            @pl.when(z > 0)
+            def _():
+                falling.wait_send()
+
+            for step in range(1, line):
+                beside, onward = other_onward(buf, turn, order(step), piece)
+
+                @pl.when(onward)
+                def _():
+                    beside.wait_send()
+
 
     for piece in range(PIECES):
         gather_start(rows_buf, 0, piece)
@@ -420,6 +482,9 @@
             [w_buf[d * PAIR + part, pl.ds(me, 1), :] for part in range(PAIR)], axis=1
         )
 
+    def place_of(step):
+        return pl.ds(step * pair_rows, pair_rows)
+
     def pair_of(d):
         return pl.ds(pl.multiple_of(d * pair_rows, pair_rows), pair_rows)
 
@@ -447,8 +512,8 @@
 
     def forward(step):
         d = order(step)
-        where = pair_of(d)
-        rows = rows_buf[where, :]
+        where = place_of(step)
+        rows = rows_buf[pair_of(d), :]
 
         def product(table):
             return lax.dot_general(table[...], rows, ROW_BY_ROW, preferred_element_type=F32)
@@ -515,41 +580,58 @@
             if step:
                 z_copy(d, piece).wait_send()
 
+    quarter = width // data_devices
+    x_of = (1 - x_at, x_at)
+    early = (line - 1) * pair_rows
+
+    def columns_of(q):
+        return pl.ds(pl.multiple_of(q * quarter, quarter), quarter)
+
     def cotangents(step):
         d = order(step)
         errors = jnp.concatenate([err_buf[d * PAIR + part] for part in range(PAIR)], axis=1)
-        cot[:, pair_of(d)] = (pair_weights(d) * errors.astype(F32)).astype(BF16)
+        cot[:, place_of(step)] = (pair_weights(d) * errors.astype(F32)).astype(BF16)
 
     def hidden_grads(step):
-        where = pair_of(order(step))
+        where = place_of(step)
         grad_hidden = jnp.dot(edown[...], cot[:, where], preferred_element_type=F32)
         gate_values = pre_gate[:, where]
         gate_sigmoid = jax.nn.sigmoid(gate_values)
-        grad_pre_gate[:, where] = (
+        there = pair_of(order(step))
+        grad_pre_gate[:, there] = (
             grad_hidden
             * pre_up[:, where]
             * gate_sigmoid
             * (1.0 + gate_values * (1.0 - gate_sigmoid))
         ).astype(BF16)
-        grad_pre_up[:, where] = (grad_hidden * (gate_values * gate_sigmoid)).astype(BF16)
+        grad_pre_up[:, there] = (grad_hidden * (gate_values * gate_sigmoid)).astype(BF16)
+
+    def down_part(q, first, count):
+        span_of = pl.ds(first, count)
+        return lax.dot_general(
+            hidden[:, span_of],
+            cot[columns_of(q), span_of],
+            ROW_BY_ROW,
+            preferred_element_type=F32,
+        )
 
     def backward(step):
         cotangents(step)
         if step < line - 1:
             hidden_grads(step)
+        if step == line - 2:
+            for slot in range(PAIR):
+                for side in range(PAIR):
+                    down_early[slot, side] = down_part(x_of[slot] * PAIR + side, 0, early)
 
     gather_rest(err_buf, 1, backward)
 
-    quarter = width // data_devices
-
-    def part(which, q):
-        columns = pl.ds(pl.multiple_of(q * quarter, quarter), quarter)
+    def part(which, slot, side):
+        q = x_of[slot] * PAIR + side
         if which == 2:
-            return lax.dot_general(
-                hidden[...], cot[columns, :], ROW_BY_ROW, preferred_element_type=F32
-            )
+            return down_early[slot, side] + down_part(q, early, pair_rows)
         grads = grad_pre_gate if which == 0 else grad_pre_up
-        return jnp.dot(grads[...], rows_buf[:, columns], preferred_element_type=F32)
+        return jnp.dot(grads[...], rows_buf[:, columns_of(q)], preferred_element_type=F32)
 
     def core_copy(which, slot):
         return remote(
@@ -568,8 +650,6 @@
             x_rsem.at[which],
             x_peer,
         )
-
-    x_of = (1 - x_at, x_at)
 
     def join(which, slot):
         core_copy(which, slot).wait_recv()
@@ -582,12 +662,13 @@
 
     items = [(which, slot) for slot in range(PAIR) for which in (2, 0, 1)]
     for at, (which, slot) in enumerate(items):
-        core_send[which, slot] = part(which, x_of[slot] * PAIR + 1 - core).astype(BF16)
+        core_send[which, slot] = part(which, slot, 1 - core).astype(BF16)
         core_copy(which, slot).start()
-        keep[which, slot] = part(which, x_of[slot] * PAIR + core)
+        keep[which, slot] = part(which, slot, core)
         if at == 0:
             hidden_grads(line - 1)
-        if at:
+            join(which, slot)
+        elif at > 1:
             join(*items[at - 1])
     join(*items[-1])
     for which, out in enumerate((out_gate, out_up, out_down)):
@@ -658,6 +739,7 @@
             pltpu.VMEM((3, PAIR) + tall, BF16),
             pltpu.VMEM((3, PAIR) + tall, BF16),
             pltpu.VMEM((3, PAIR) + tall, F32),
+            pltpu.VMEM((PAIR, PAIR) + tall, F32),
             pltpu.VMEM((3,) + tall, BF16),
             pltpu.VMEM((3,) + tall, BF16),
             dma((6,)),
@@ -666,6 +748,7 @@
             dma((2, peers, PIECES)),
             dma((2, line, PIECES)),
             dma((2, line + 1, PIECES)),
+            dma((2, line + 1, Y_FIRST)),
             dma((line, PIECES)),
             dma((line, PIECES)),
             dma((line, PIECES)),

time: 124 us -> 121 us (0.976)
  Pallas kernels: 119 us -> 116 us
    pallas_call x1, Pallas kernels: 119 us -> 116 us  [fused_on_device(): pl.pallas_call(functools.partial(fused_kernel, line, data_devices, loss_s...]
where the time goes in v4:
time: 121 us; the launch traced here: 120 us
  Pallas kernels  116 us (96%)
  local copies, waits for them, and re-layouts  3.85 us (3%)
    pallas_call x1, Pallas kernels, fused_on_device(): pl.pallas_call(functools.partial(fused_kernel, line, data_devices, loss_s...  116 us
    unnamed x7, local copies, waits for them, and re-layouts  3.85 us

profile of v4, /device:TPU:0, one launch (start us, length us, event | category | flops | bytes accessed | tf_op | source)
XLA Modules:
  0.0 120.4 jit_solution(17401508859761174793)
XLA Ops:
  0.6 115.9 %shard_map.112 = (f32[1,704,256]{2,1,0:T(8,128)}, f32[1,704,256]{2,1,0:T(8,128)}, f32[1,704,256]{2,1,0:T(8,128)}) custom-call(bf16[128,1024]{1,0:T(8,128)(2,1)} %tokens_ref.1, f32[8,1024]{1,0:T(8,128)} %bitcast.14, s32[4,128]{1,0:T(4,128)} %bitcast.15, bf16[344,1024]{1,0:T(8,128)(2,1)} %bitcast.12, bf16[344,1024]{1,0:T(8,128)(2,1)} %bitcast.13, ...), custom_call_target="tpu_custom_call" | custom-call | flops 12499025920 | bytes 5767168 | tf_op jit(solution)/shard_map/pallas_call | solution.py:711
  116.5 0.0 copy-start.1
  116.5 0.0 copy-start
  116.6 2.1 %copy.15 = f32[1,256,704]{1,2,0:T(8,128)} copy(f32[1,256,704]{1,2,0:T(8,128)} %bitcast.9) | data formatting | bytes 1441792
  118.7 0.0 copy-done.1
  118.7 0.9 copy.16
  119.5 0.0 copy-done
  119.5 0.9 copy.17
Async XLA Ops:
  116.5 2.1 %copy-start.1 = (f32[1,704,256]{2,1,0:T(8,128)S(1)}, f32[1,704,256]{2,1,0:T(8,128)}, u32[]{:S(2)}) copy-start(f32[1,704,256]{2,1,0:T(8,128)} %get-tuple-element.7) | copy-start | bytes 2162692
  116.5 3.0 %copy-start = (f32[1,704,256]{2,1,0:T(8,128)S(1)}, f32[1,704,256]{2,1,0:T(8,128)}, u32[]{:S(2)}) copy-start(f32[1,704,256]{2,1,0:T(8,128)} %get-tuple-element.14) | copy-start | bytes 2162692

commit v5 on v4

--- a/solution.py
+++ b/solution.py
@@ -179,9 +179,8 @@
     gate_hbm,
     up_hbm,
     down_hbm,
-    out_gate,
-    out_up,
-    out_down,
+    own_out,
+    x_recv,
     tgate,
     tup,
     tdown,
@@ -209,7 +208,9 @@
     keep,
     down_early,
     x_send,
-    x_recv,
+    z_pass,
+    own_sem,
+    pass_rsem,
     load_sem,
     w_ssem,
     w_rsem,
@@ -510,6 +511,21 @@
             (dp, d * PAIR + y),
         )
 
+    passing = line >= 4
+    at_end = jnp.logical_or(z == 0, z == line - 1)
+
+    def pass_copy(d, piece):
+        rising = d > z
+        way = jnp.where(rising, 0, 1)
+        part_rows = pl.ds(piece * span, span)
+        return remote(
+            z_send.at[d, part_rows],
+            z_pass.at[way, part_rows],
+            rs_zsem.at[d, piece],
+            pass_rsem.at[way, piece],
+            (dp, jnp.where(rising, me + PAIR, me - PAIR)),
+        )
+
     def forward(step):
         d = order(step)
         where = place_of(step)
@@ -545,11 +561,30 @@
         at = pl.ds(piece * span, span)
         y_copy(d, piece).wait_recv()
         total = part_own[d, at] + y_recv[d, at].astype(F32)
-        if step:
+        if step == 0:
+            part_own[d, at] = total
+        elif step < line - 1 or not passing:
             z_send[d, at] = total.astype(BF16)
             z_copy(d, piece).start()
         else:
-            part_own[d, at] = total
+            handed = jnp.logical_or(z == 1, z == line - 2)
+
+            @pl.when(at_end)
+            def _():
+                z_send[d, at] = total.astype(BF16)
+                pass_copy(d, piece).start()
+
+            @pl.when(handed)
+            def _():
+                pass_copy(d, piece).wait_recv()
+                way = jnp.where(d > z, 0, 1)
+                z_send[d, at] = (total + z_pass[way, at].astype(F32)).astype(BF16)
+                z_copy(d, piece).start()
+
+            @pl.when(jnp.logical_not(jnp.logical_or(at_end, handed)))
+            def _():
+                z_send[d, at] = total.astype(BF16)
+                z_copy(d, piece).start()
 
     gather_rest(rows_buf, 0, forward)
     for piece in range(PIECES):
@@ -558,18 +593,24 @@
         combine(0, piece)
     for piece in range(PIECES):
         at = pl.ds(piece * span, span)
-        total = part_own[z, at]
         for step in range(1, line):
-            d = order(step)
-            remote(
-                z_send.at[d, at],
-                z_recv.at[d, at],
-                rs_zsem.at[d, piece],
-                rs_zrsem.at[d, piece],
-                y_peer,
-            ).wait_recv()
-            total += z_recv[d, at].astype(F32)
-        err_buf[me, at] = (total * loss_scale).astype(BF16)
+            source = order(step)
+
+            def take():
+                remote(
+                    z_send.at[source, at],
+                    z_recv.at[source, at],
+                    rs_zsem.at[source, piece],
+                    rs_zrsem.at[source, piece],
+                    y_peer,
+                ).wait_recv()
+                part_own[z, at] += z_recv[source, at].astype(F32)
+
+            if step == line - 1 and passing:
+                pl.when(jnp.logical_not(at_end))(take)
+            else:
+                take()
+        err_buf[me, at] = (part_own[z, at] * loss_scale).astype(BF16)
         gather_start(err_buf, 1, piece)
 
     gather_drain(rows_buf, 0)
@@ -651,6 +692,9 @@
             x_peer,
         )
 
+    def own_copy(which):
+        return pltpu.make_async_copy(keep.at[which, 1], own_out.at[which], own_sem.at[which])
+
     def join(which, slot):
         core_copy(which, slot).wait_recv()
         total = keep[which, slot] + core_recv[which, slot].astype(F32)
@@ -659,6 +703,7 @@
             x_copy(which).start()
         else:
             keep[which, slot] = total
+            own_copy(which).start()
 
     items = [(which, slot) for slot in range(PAIR) for which in (2, 0, 1)]
     for at, (which, slot) in enumerate(items):
@@ -671,12 +716,10 @@
         elif at > 1:
             join(*items[at - 1])
     join(*items[-1])
-    for which, out in enumerate((out_gate, out_up, out_down)):
-        x_copy(which).wait_recv()
-        out[0] = keep[which, 1] + x_recv[which].astype(F32)
     gather_drain(err_buf, 1)
     for which in range(3):
-        x_copy(which).wait_send()
+        own_copy(which).wait()
+        x_copy(which).wait()
         for slot in range(PAIR):
             core_copy(which, slot).wait_send()
 
@@ -708,11 +751,14 @@
     flops = 2 * group * width * (3 * teacher_gate.shape[1] + 7 * units)
     tall = (units, quarter)
     dma = pltpu.SemaphoreType.DMA
-    grad_gate, grad_up, grad_down = pl.pallas_call(
+    own, arrived = pl.pallas_call(
         functools.partial(fused_kernel, line, data_devices, loss_scale),
-        out_shape=(jax.ShapeDtypeStruct((1,) + tall, F32),) * 3,
+        out_shape=(
+            jax.ShapeDtypeStruct((3,) + tall, F32),
+            jax.ShapeDtypeStruct((3,) + tall, BF16),
+        ),
         in_specs=[vmem] * 3 + [hbm] * 6,
-        out_specs=(vmem,) * 3,
+        out_specs=(hbm,) * 2,
         scratch_shapes=[
             pltpu.VMEM(teacher_gate.shape[::-1], BF16),
             pltpu.VMEM(teacher_up.shape[::-1], BF16),
@@ -741,7 +787,9 @@
             pltpu.VMEM((3, PAIR) + tall, F32),
             pltpu.VMEM((PAIR, PAIR) + tall, F32),
             pltpu.VMEM((3,) + tall, BF16),
-            pltpu.VMEM((3,) + tall, BF16),
+            pltpu.VMEM((2, width, tok_count), BF16),
+            dma((3,)),
+            dma((2, PIECES)),
             dma((6,)),
             dma((peers - 1,)),
             dma((peers - 1,)),
@@ -775,7 +823,8 @@
         jnp.swapaxes(expert_up, 1, 2),
         expert_down,
     )
-    return (jnp.swapaxes(grad_gate, 1, 2), jnp.swapaxes(grad_up, 1, 2), grad_down)
+    grads = [own[at : at + 1] + arrived[at : at + 1].astype(F32) for at in range(3)]
+    return (jnp.swapaxes(grads[0], 1, 2), jnp.swapaxes(grads[1], 1, 2), grads[2])
 
 
 def fits_kernel(mesh):

time: 121 us -> 118 us (0.975)
  local copies, waits for them, and re-layouts: 3.85 us -> 0 us
  other arithmetic: 0 us -> 3.26 us
  Pallas kernels: 116 us -> 114 us
    unnamed x7 -> x0, local copies, waits for them, and re-layouts: 3.85 us -> none
    add x0 -> x1, other arithmetic: none -> 3.26 us  [fused_on_device(): grads = [own[at:at + 1] + arrived[at:at + 1].astype(F32) for at in range(3)]]
    pallas_call x1, Pallas kernels: 116 us -> 114 us  [fused_on_device(): pl.pallas_call(functools.partial(fused_kernel, line, data_devices, loss_s...]
where the time goes in v5:
time: 118 us
  Pallas kernels  114 us (97%)
  other arithmetic  3.26 us (3%)
    pallas_call x1, Pallas kernels, fused_on_device(): pl.pallas_call(functools.partial(fused_kernel, line, data_devices, loss_s...  114 us
    add x1, other arithmetic, fused_on_device(): grads = [own[at:at + 1] + arrived[at:at + 1].astype(F32) for at in range(3)]  3.26 us

profile of v5, /device:TPU:0, one launch (start us, length us, event | category | flops | bytes accessed | tf_op | source)
XLA Modules:
  0.0 117.8 jit_solution(15988652711480628702)
XLA Ops:
  0.6 113.9 %shard_map.112 = (f32[3,704,256]{2,1,0:T(8,128)}, bf16[3,704,256]{2,1,0:T(8,128)(2,1)}) custom-call(bf16[128,1024]{1,0:T(8,128)(2,1)} %tokens_ref.1, f32[8,1024]{1,0:T(8,128)} %bitcast.14, s32[4,128]{1,0:T(4,128)} %bitcast.15, bf16[344,1024]{1,0:T(8,128)(2,1)} %bitcast.12, bf16[344,1024]{1,0:T(8,128)(2,1)} %bitcast.13, bf16[344,1024]{1,0:T(8,128)(2,1)} %tdown_hbm.1, ...), custom_call_target="tpu_custom_call" | custom-call | flops 12499025920 | bytes 5767168 | tf_op jit(solution)/shard_map/pallas_call | solution.py:754
  114.6 3.3 %convert_add_fusion = (f32[1,704,256]{2,1,0:T(8,128)}, f32[1,256,704]{1,2,0:T(8,128)}, f32[1,256,704]{1,2,0:T(8,128)}) fusion(f32[3,704,256]{2,1,0:T(8,128)} %get-tuple-element.5, bf16[3,704,256]{2,1,0:T(8,128)(2,1)} %get-tuple-element.6), kind=kLoop, calls=%fused_computation | loop fusion | flops 1081344 | bytes 5406720 | tf_op jit(solution)/shard_map/add | solution.py:826

commit v6 on v5

--- a/solution.py
+++ b/solution.py
@@ -155,8 +155,8 @@
 
 
 PAIR = 2
-PIECES = 4
-Y_FIRST = 1
+PIECES = 8
+Y_FIRST = 2
 ROW_BY_ROW = (((1,), (1,)), ((), ()))
 BF16 = jnp.bfloat16
 F32 = jnp.float32

time: 118 us -> 119 us (level)
  no operation moved by 1% of the time
where the time goes in v6:
time: 119 us
  Pallas kernels  115 us (97%)
  other arithmetic  3.26 us (3%)
    pallas_call x1, Pallas kernels, fused_on_device(): pl.pallas_call(functools.partial(fused_kernel, line, data_devices, loss_s...  115 us
    add x1, other arithmetic, fused_on_device(): grads = [own[at:at + 1] + arrived[at:at + 1].astype(F32) for at in range(3)]  3.26 us

profile of v6, /device:TPU:0, one launch (start us, length us, event | category | flops | bytes accessed | tf_op | source)
XLA Modules:
  0.0 118.8 jit_solution(10849650727554604699)
XLA Ops:
  0.6 114.9 %shard_map.112 = (f32[3,704,256]{2,1,0:T(8,128)}, bf16[3,704,256]{2,1,0:T(8,128)(2,1)}) custom-call(bf16[128,1024]{1,0:T(8,128)(2,1)} %tokens_ref.1, f32[8,1024]{1,0:T(8,128)} %bitcast.14, s32[4,128]{1,0:T(4,128)} %bitcast.15, bf16[344,1024]{1,0:T(8,128)(2,1)} %bitcast.12, bf16[344,1024]{1,0:T(8,128)(2,1)} %bitcast.13, bf16[344,1024]{1,0:T(8,128)(2,1)} %tdown_hbm.1, ...), custom_call_target="tpu_custom_call" | custom-call | flops 12499025920 | bytes 5767168 | tf_op jit(solution)/shard_map/pallas_call | solution.py:754
  115.6 3.3 %convert_add_fusion = (f32[1,704,256]{2,1,0:T(8,128)}, f32[1,256,704]{1,2,0:T(8,128)}, f32[1,256,704]{1,2,0:T(8,128)}) fusion(f32[3,704,256]{2,1,0:T(8,128)} %get-tuple-element.5, bf16[3,704,256]{2,1,0:T(8,128)(2,1)} %get-tuple-element.6), kind=kLoop, calls=%fused_computation | loop fusion | flops 1081344 | bytes 5406720 | tf_op jit(solution)/shard_map/add | solution.py:826
